TPU v7x, 32 devices: a whole 2x2x4 slice. The times are simulated.
32 devices in a mesh: dp: 2 (over x), row: 4 (over y, core), col: 4 (over z).
Axes of the slice: x: 2, y: 2, z: 4, core: 2. Of those that a mesh axis runs over, the one named last changes fastest.
Arguments:
- residual_in: float32 [12288, 1280], P(('dp', 'row'), 'col'), may hold values from -6 to 6
- seq_ids: int32 [12288], P('dp'), may hold values from 0 to 3, as said below
- norm1_gain: float32 [1280], P('col'), may hold values from 0.1 to 1.9
- w_qkv: float32 [1280, 3, 1280], P('row', None, 'col'), may hold values from -0.15625 to 0.15625
- per_dim: float32 [80], replicated, may hold values from 0 to 1.5
- w_out: float32 [1280, 1280], P('col', 'row'), may hold values from -1.25 to 1.25
- norm2_gain: float32 [1280], P('col'), may hold values from 0.1 to 1.9
- w_up: float32 [1280, 1280], P('row', 'col'), may hold values from -0.15625 to 0.15625
- w_down: float32 [1280, 1280], P('col', 'row'), may hold values from -0.15625 to 0.15625
- out_grad: float32 [12288, 1280], P(('dp', 'row'), 'col'), may hold values from -6 to 6
Outputs:
- output: float32 [12288, 1280], P(('dp', 'row'), 'col')
- input_grad: float32 [12288, 1280], P(('dp', 'row'), 'col')
- norm1_gain_grad: float32 [1280], P('col')
- w_qkv_grad: float32 [1280, 3, 1280], P('row', None, 'col')
- per_dim_grad: float32 [80], replicated
- w_out_grad: float32 [1280, 1280], P('col', 'row')
- norm2_gain_grad: float32 [1280], P('col')
- w_up_grad: float32 [1280, 1280], P('row', 'col')
- w_down_grad: float32 [1280, 1280], P('col', 'row')
Inputs may be any that keep to these rules, and one draw needn't show every extreme that they name: seq_ids never fall; the 6144 tokens of one index g of dp hold exactly 2 sequences, numbered g * 2 to g * 2 + 1; each sequence starts at a multiple of 256 tokens within the group and has at least 768 tokens.
All inputs are finite; a program needn't handle non-finite values.
Results may differ from a plain program's by a relative error of at most 0.017.
The roundings to bfloat16 on the way count: a program that leaves them out, or rounds other values in their place, can miss the bound.
Values may be sent and summed in bfloat16 or wider, within the bound.
No kernel may reach another device: no remote copies, remote signals or barrier semaphores. Data moves between devices by JAX's collectives and lax.ppermute only.
A program may use at most 320 MiB of HBM per device.

v0:
```python
from functools import reduce
import math

import jax
import jax.numpy as jnp
from jax import lax
from jax.sharding import PartitionSpec as P

D = 1280
HD = 80
LEN = 3072
BLK = 256


epsilon = 1e-06
scale_base = 1.442695041
masked = -1e30


def scores_for(queries, keys, query_pos, key_pos, query_seq, key_seq):
    dense = jnp.einsum("qd,kd->qk", queries, keys, preferred_element_type=jnp.float32)
    allowed = (query_seq[:, None] == key_seq[None, :]) & (
        key_pos[None, :] // BLK <= query_pos[:, None] // BLK
    )
    return jnp.where(allowed, dense, masked)


def normalize(values, norm_gain):
    totals = lax.psum(jnp.sum(values * values, axis=1), "col")
    inverse = lax.rsqrt(totals / D + epsilon)[:, None]
    return (inverse, (values * inverse * norm_gain).astype(jnp.bfloat16))


def features(values):
    return lax.all_gather(values, "col", axis=1, tiled=True)


def branch_total(values):
    return lax.psum_scatter(values, "col", scatter_dimension=1, tiled=True)


def grads_in(values):
    return lax.all_gather(values, "col", axis=1, tiled=True)


def grads_out(values):
    return lax.psum_scatter(values, "col", scatter_dimension=1, tiled=True)


def norm_back(values, inverse, norm_gain, incoming, extra):
    scaled = norm_gain * incoming
    summed = lax.psum((jnp.sum(scaled * values, axis=1),) + extra, "col")
    result = inverse * scaled - values * inverse**3 * summed[0][:, None] / D
    gain_part = jnp.sum(incoming * values * inverse, axis=0)
    return (result, gain_part, summed[1:])


def split_heads(values, head_count):
    return values.reshape(values.shape[0], head_count, HD).transpose(1, 0, 2)


def merge_heads(values):
    return values.transpose(1, 0, 2).reshape(values.shape[1], values.shape[0] * HD)


def block_terms(
    block_q, block_go, block_lse, block_pos, block_seq, head_k, head_v, seq_ids, span_count
):
    weights = []
    slopes = []
    for piece in range(span_count):
        lower = piece * LEN
        scores = scores_for(
            block_q,
            head_k[lower : lower + LEN],
            block_pos,
            lower + jnp.arange(LEN),
            block_seq,
            seq_ids[lower : lower + LEN],
        )
        weights.append(jnp.exp(scores - block_lse[:, None]))
        slopes.append(
            jnp.einsum(
                "qd,kd->qk",
                block_go,
                head_v[lower : lower + LEN],
                preferred_element_type=jnp.float32,
            )
        )
    deltas = reduce(
        jnp.add,
        [
            jnp.sum(weight_piece * slope_piece, axis=1)
            for weight_piece, slope_piece in zip(weights, slopes)
        ],
    )
    score_grads = [
        (weight_piece * (slope_piece - deltas[:, None])).astype(jnp.bfloat16)
        for weight_piece, slope_piece in zip(weights, slopes)
    ]
    grad_q = reduce(
        jnp.add,
        [
            jnp.dot(
                score_grads[piece],
                head_k[piece * LEN : (piece + 1) * LEN],
                preferred_element_type=jnp.float32,
            )
            for piece in range(span_count)
        ],
    )
    return (weights, score_grads, grad_q, deltas)


def on_device(
    residual_in, seq_ids, norm1_gain, w_qkv, per_dim, w_out, norm2_gain, w_up, w_down, out_grad
):
    row_count, feature_width = residual_in.shape
    local_heads = feature_width // HD
    group_size = seq_ids.shape[0]
    span_count = group_size // LEN
    block_count = max(1, row_count // 1024)
    first_row = lax.axis_index("row") * row_count
    query_pos = first_row + jnp.arange(row_count)
    query_seq = lax.dynamic_slice_in_dim(seq_ids, first_row, row_count)
    copies = (
        w_qkv.astype(jnp.bfloat16),
        w_out.astype(jnp.bfloat16),
        w_up.astype(jnp.bfloat16),
        w_down.astype(jnp.bfloat16),
    )
    qkv_copy, out_copy, up_copy, down_copy = (
        lax.all_gather(copies[0], "row", axis=0, tiled=True),
        lax.all_gather(copies[1], "row", axis=1, tiled=True),
        lax.all_gather(copies[2], "row", axis=0, tiled=True),
        lax.all_gather(copies[3], "row", axis=1, tiled=True),
    )
    inverse_one, normed_one = normalize(residual_in, norm1_gain)
    normed_all = features(normed_one)
    projected = jnp.einsum("rd,dtc->rtc", normed_all, qkv_copy, preferred_element_type=jnp.float32)
    scale = jax.nn.softplus(per_dim) * scale_base / math.sqrt(HD)
    scale_row = jnp.tile(scale, local_heads)
    queries = (projected[:, 0] * scale_row).astype(jnp.bfloat16)
    key_value = projected[:, 1:].astype(jnp.bfloat16)
    key_value_all = lax.all_gather(key_value, "row", axis=0, tiled=True)
    query_heads = split_heads(queries, local_heads)
    key_heads = split_heads(key_value_all[:, 0], local_heads)
    value_heads = split_heads(key_value_all[:, 1], local_heads)

    def forward_head(operands):
        head_q, head_k, head_v = operands

        def forward_one_block(carried, number):
            scores = [
                scores_for(
                    head_q,
                    head_k[piece * LEN : (piece + 1) * LEN],
                    query_pos,
                    piece * LEN + jnp.arange(LEN),
                    query_seq,
                    seq_ids[piece * LEN : (piece + 1) * LEN],
                )
                for piece in range(span_count)
            ]
            maxima = reduce(jnp.maximum, [jnp.max(piece_scores, axis=1) for piece_scores in scores])
            totals = reduce(
                jnp.add,
                [
                    jnp.sum(jnp.exp(piece_scores - maxima[:, None]), axis=1)
                    for piece_scores in scores
                ],
            )
            log_totals = maxima + jnp.log(totals)
            result = reduce(
                jnp.add,
                [
                    jnp.dot(
                        jnp.exp(scores[piece] - log_totals[:, None]).astype(jnp.bfloat16),
                        head_v[piece * LEN : (piece + 1) * LEN],
                        preferred_element_type=jnp.float32,
                    )
                    for piece in range(span_count)
                ],
            )
            return (carried, (result, log_totals))

        leftover, (result, log_totals) = lax.scan(
            forward_one_block, jnp.int32(0), jnp.arange(block_count)
        )
        return (result.reshape(row_count, HD), log_totals.reshape(row_count))

    attended_heads, log_totals = lax.map(forward_head, (query_heads, key_heads, value_heads))
    attended = merge_heads(attended_heads).astype(jnp.bfloat16)
    middle = residual_in + branch_total(
        jnp.dot(attended, out_copy, preferred_element_type=jnp.float32)
    )
    inverse_two, normed_two = normalize(middle, norm2_gain)
    normed_all_two = features(normed_two)
    up_proj = jnp.dot(normed_all_two, up_copy, preferred_element_type=jnp.float32)
    activated = jax.nn.silu(up_proj).astype(jnp.bfloat16)
    output = middle + branch_total(
        jnp.dot(activated, down_copy, preferred_element_type=jnp.float32)
    )
    grad_mlp = grads_in(out_grad.astype(jnp.bfloat16))
    down_part = jnp.einsum("rf,rd->fd", activated, grad_mlp, preferred_element_type=jnp.float32)
    grad_act = jnp.einsum("rd,fd->rf", grad_mlp, down_copy, preferred_element_type=jnp.float32)
    sigmoid_up = jax.nn.sigmoid(up_proj)
    grad_up = (grad_act * sigmoid_up * (1.0 + up_proj * (1.0 - sigmoid_up))).astype(jnp.bfloat16)
    up_part = jnp.einsum("rd,rf->df", normed_all_two, grad_up, preferred_element_type=jnp.float32)
    grad_two = grads_out(
        jnp.einsum("rf,df->rd", grad_up, up_copy, preferred_element_type=jnp.float32)
    )
    back_two, gain_two_part, unused_two = norm_back(middle, inverse_two, norm2_gain, grad_two, ())
    grad_middle = out_grad + back_two
    grad_branch = grads_in(grad_middle.astype(jnp.bfloat16))
    out_part = jnp.einsum("rc,rd->cd", attended, grad_branch, preferred_element_type=jnp.float32)
    grad_attended = jnp.einsum(
        "rd,cd->rc", grad_branch, out_copy, preferred_element_type=jnp.float32
    ).astype(jnp.bfloat16)
    grad_heads = split_heads(grad_attended, local_heads)

    def backward_head(operands):
        head_q, head_k, head_v, head_go, head_lse = operands

        def backward_one_block(carried, number):
            acc_k, acc_v = carried
            weights, score_grads, grad_q, deltas = block_terms(
                head_q, head_go, head_lse, query_pos, query_seq, head_k, head_v, seq_ids, span_count
            )
            new_k = jnp.concatenate(
                [
                    jnp.einsum("qk,qd->kd", piece_grads, head_q, preferred_element_type=jnp.float32)
                    for piece_grads in score_grads
                ],
                axis=0,
            )
            new_v = jnp.concatenate(
                [
                    jnp.einsum(
                        "qk,qd->kd",
                        weight_piece.astype(jnp.bfloat16),
                        head_go,
                        preferred_element_type=jnp.float32,
                    )
                    for weight_piece in weights
                ],
                axis=0,
            )
            return ((acc_k + new_k, acc_v + new_v), grad_q)

        zeros = jnp.zeros((group_size, HD), jnp.float32)
        (acc_k, acc_v), grad_q = lax.scan(
            backward_one_block, (zeros, zeros), jnp.arange(block_count)
        )
        return (grad_q.reshape(row_count, HD), acc_k, acc_v)

    grad_q_heads, key_grads_all, value_grads_all = lax.map(
        backward_head, (query_heads, key_heads, value_heads, grad_heads, log_totals)
    )
    grad_keys, grad_values = (
        lax.psum_scatter(
            merge_heads(key_grads_all).astype(jnp.bfloat16), "row", scatter_dimension=0, tiled=True
        ).astype(jnp.float32),
        lax.psum_scatter(
            merge_heads(value_grads_all).astype(jnp.bfloat16),
            "row",
            scatter_dimension=0,
            tiled=True,
        ).astype(jnp.float32),
    )
    grad_scaled = merge_heads(grad_q_heads)
    scale_part = (
        jnp.sum((grad_scaled * projected[:, 0]).reshape(row_count, local_heads, HD), axis=(0, 1))
        * (scale_base / math.sqrt(HD))
        * jax.nn.sigmoid(per_dim)
    )
    grad_projected = jnp.stack([grad_scaled * scale_row, grad_keys, grad_values], axis=1).astype(
        jnp.bfloat16
    )
    qkv_part = jnp.einsum(
        "rd,rtc->dtc", normed_all, grad_projected, preferred_element_type=jnp.float32
    )
    grad_one = grads_out(
        jnp.einsum("rtc,dtc->rd", grad_projected, qkv_copy, preferred_element_type=jnp.float32)
    )
    back_one, gain_one_part, extras = norm_back(
        residual_in, inverse_one, norm1_gain, grad_one, (scale_part,)
    )
    input_grad = grad_middle + back_one
    shards = (
        lax.psum_scatter(
            qkv_part.astype(jnp.bfloat16), "row", scatter_dimension=0, tiled=True
        ).astype(jnp.float32),
        lax.psum_scatter(
            out_part.astype(jnp.bfloat16), "row", scatter_dimension=1, tiled=True
        ).astype(jnp.float32),
        lax.psum_scatter(
            up_part.astype(jnp.bfloat16), "row", scatter_dimension=0, tiled=True
        ).astype(jnp.float32),
        lax.psum_scatter(
            down_part.astype(jnp.bfloat16), "row", scatter_dimension=1, tiled=True
        ).astype(jnp.float32),
    )
    qkv_grad, out_grad_w, up_grad, down_grad = (
        lax.psum(shards[0].astype(jnp.bfloat16), "dp").astype(jnp.float32),
        lax.psum(shards[1].astype(jnp.bfloat16), "dp").astype(jnp.float32),
        lax.psum(shards[2].astype(jnp.bfloat16), "dp").astype(jnp.float32),
        lax.psum(shards[3].astype(jnp.bfloat16), "dp").astype(jnp.float32),
    )
    gain_one_grad, gain_two_grad, scale_grad = lax.psum(
        (gain_one_part, gain_two_part, extras[0]), ("dp", "row")
    )
    return (
        output,
        input_grad,
        gain_one_grad,
        qkv_grad,
        scale_grad,
        out_grad_w,
        gain_two_grad,
        up_grad,
        down_grad,
    )


def solution(mesh):
    in_specs = (
        P(("dp", "row"), "col"),
        P("dp"),
        P("col"),
        P("row", None, "col"),
        P(),
        P("col", "row"),
        P("col"),
        P("row", "col"),
        P("col", "row"),
        P(("dp", "row"), "col"),
    )
    out_specs = (
        P(("dp", "row"), "col"),
        P(("dp", "row"), "col"),
        P("col"),
        P("row", None, "col"),
        P(),
        P("col", "row"),
        P("col"),
        P("row", "col"),
        P("col", "row"),
    )
    return jax.shard_map(
        on_device, mesh=mesh, in_specs=in_specs, out_specs=out_specs, check_vma=False
    )
```

profile of v0, /device:TPU:0, one launch (start us, length us, event | category | flops | bytes accessed | tf_op | source)
XLA Modules:
  0.0 1976.5 jit_solution(12522214331487185538)
XLA Ops:
  10.7 13.7 psum.84
  26.8 19.4 all-gather.9.cloned.1.call-done
  46.3 78.6 %all-gather.7.cloned.1.call-done = bf16[1536,1280]{0,1:T(8,128)(2,1)} async-done(((bf16[1536,320]{0,1:T(8,128)(2,1)}), bf16[1536,1280]{0,1:T(8,128)(2,1)}) %all-gather.7.cloned.1.call-update) | async-done | bytes 3932176 | tf_op jit(solution)/shard_map/all_gather | solution.py:35
  137.8 10.2 all_gather.30
  152.1 38.6 %all-gather.11.cloned.1.call-done = bf16[6144,2,320]{0,2,1:T(8,128)(2,1)} async-done(((bf16[1536,2,320]{0,2,1:T(8,128)(2,1)}), bf16[6144,2,320]{0,2,1:T(8,128)(2,1)}) %all-gather.11.cloned.1.call-update) | async-done | bytes 7864336 | tf_op jit(solution)/shard_map/all_gather | solution.py:145
  211.5 188.8 %while.49 = (s32[]{:T(128)}, bf16[4,1536,80]{1,2,0:T(8,128)(2,1)S(1)}, f32[4,1536]{1,0:T(4,128)}, s32[1536]{0:T(1024)S(1)}, s32[6144]{0:T(1024)}, /*index=5*/bf1...) while((s32[]{:T(128)}, ...), condition=%wide.region_7.8_spmd.clone.clone.clone, body=%wide.region_2.7_spmd.clone.clone.sunk.clone | while | flops 3105056256 | bytes 194444432 | solution.py:192
  217.7 11.7 fusion.185
  229.9 9.2 exponential_reduce_fusion.4
  239.2 8.5 fusion.186
  247.6 9.6 fusion.187
  264.7 11.7 fusion.185
  276.9 9.2 exponential_reduce_fusion.4
  286.1 8.5 fusion.186
  294.6 9.7 fusion.187
  311.7 11.7 fusion.185
  323.9 9.2 exponential_reduce_fusion.4
  333.1 8.5 fusion.186
  341.6 9.7 fusion.187
  358.8 11.7 fusion.185
  370.9 9.2 exponential_reduce_fusion.4
  388.6 9.8 fusion.187
  405.7 136.3 %reduce-scatter.15.cloned.1.call-done = f32[1536,320]{0,1:T(8,128)} async-done(((f32[1536,1280]{0,1:T(8,128)}), f32[1536,320]{0,1:T(8,128)}) %reduce-scatter.15.cloned.1.call-update) | async-done | bytes 1966096 | tf_op jit(solution)/shard_map/reduce_scatter | solution.py:39
  545.2 11.8 psum.85
  563.9 10.3 all_gather.33
  574.2 9.8 all_gather.32
  584.0 51.4 %all-gather.13.cloned.1.call-done = bf16[1536,1280]{0,1:T(8,128)(2,1)} async-done(((bf16[1536,320]{0,1:T(8,128)(2,1)}), bf16[1536,1280]{0,1:T(8,128)(2,1)}) %all-gather.13.cloned.1.call-update) | async-done | bytes 3932176 | tf_op jit(solution)/shard_map/all_gather | solution.py:35
  640.3 72.2 %all-gather.15.cloned.1.call-done = bf16[1536,1280]{0,1:T(8,128)(2,1)} async-done(((bf16[1536,320]{0,1:T(8,128)(2,1)}), bf16[1536,1280]{0,1:T(8,128)(2,1)}) %all-gather.15.cloned.1.call-update) | async-done | bytes 3932176 | tf_op jit(solution)/shard_map/all_gather | solution.py:43
  731.2 127.0 %reduce-scatter.19.cloned.1.call-done = f32[1536,320]{0,1:T(8,128)} async-done(((f32[1536,1280]{0,1:T(8,128)}), f32[1536,320]{0,1:T(8,128)}) %reduce-scatter.19.cloned.1.call-update) | async-done | bytes 1966096 | tf_op jit(solution)/shard_map/reduce_scatter | solution.py:47
  860.9 11.9 psum.86
  872.8 124.7 %reduce-scatter.17.cloned.1.call-done = f32[1536,320]{0,1:T(8,128)} async-done(((f32[1536,1280]{0,1:T(8,128)}), f32[1536,320]{0,1:T(8,128)}) %reduce-scatter.17.cloned.1.call-update) | async-done | bytes 1966096 | tf_op jit(solution)/shard_map/reduce_scatter | solution.py:39
  1003.3 76.9 %all-gather.17.cloned.1.call-done = bf16[1536,1280]{0,1:T(8,128)(2,1)} async-done(((bf16[1536,320]{0,1:T(8,128)(2,1)}), bf16[1536,1280]{0,1:T(8,128)(2,1)}) %all-gather.17.cloned.1.call-update) | async-done | bytes 3932176 | tf_op jit(solution)/shard_map/all_gather | solution.py:43
  1086.8 452.5 %while.50 = (s32[]{:T(128)}, f32[4,1536,80]{1,2,0:T(8,128)}, bf16[4,6144,80]{1,2,0:T(8,128)(2,1)}, bf16[4,6144,80]{1,2,0:T(8,128)(2,1)}, s32[1536]{0:T(1024)S(1)...) while((s32[]{:T(128)}, f32[4,1536,80]{1,2,0:T(8,128)}, ...), condition=%wide.region_18.19_spmd.clone.clone.clone, body=%wide.region_15.18_spmd.clone.clone.sunk.clone | while | flops 7657711104 | bytes 336350880 | solution.py:257
  1087.9 9.0 fusion.200
  1096.9 17.2 multiply_reduce_fusion.12
  1122.3 8.9 fusion.202
  1131.1 17.1 multiply_reduce_fusion.13
  1148.2 28.7 %multiply_convert_fusion.10 = (bf16[1536,3072]{1,0:T(8,128)(2,1)S(1)}, bf16[1536,3072]{1,0:T(8,128)(2,1)}) fusion(f32[1536,3072]{1,0:T(8,128)} %get-tuple-element.936, f32[1536,3072]{1,0:T(8,128)} %fusion.200, f32[1536]{0:T(1024)S(1)} %add.582, f32[1536,3072]{1,0:T(8,128)} %get-tuple-element.940, f32[1536,3072]{1,0:T(8,128)} %fusion.202), kind=kLoop, calls=%fused_computation.59.clone.1.clone | loop fusion | flops 28311552 | bytes 94377984 | tf_op jit(solution)/shard_map/while/body/eval_jaxpr/while/body/eval_jaxpr/convert_element_type | solution.py:98
  1200.9 9.0 fusion.200
  1209.9 17.2 multiply_reduce_fusion.12
  1235.3 8.9 fusion.202
  1244.1 17.1 multiply_reduce_fusion.13
  1261.2 28.7 %multiply_convert_fusion.10 = (bf16[1536,3072]{1,0:T(8,128)(2,1)S(1)}, bf16[1536,3072]{1,0:T(8,128)(2,1)}) fusion(f32[1536,3072]{1,0:T(8,128)} %get-tuple-element.936, f32[1536,3072]{1,0:T(8,128)} %fusion.200, f32[1536]{0:T(1024)S(1)} %add.582, f32[1536,3072]{1,0:T(8,128)} %get-tuple-element.940, f32[1536,3072]{1,0:T(8,128)} %fusion.202), kind=kLoop, calls=%fused_computation.59.clone.1.clone | loop fusion | flops 28311552 | bytes 94377984 | tf_op jit(solution)/shard_map/while/body/eval_jaxpr/while/body/eval_jaxpr/convert_element_type | solution.py:98
  1313.9 9.0 fusion.200
  1322.9 17.2 multiply_reduce_fusion.12
  1348.3 8.9 fusion.202
  1357.2 17.1 multiply_reduce_fusion.13
  1374.3 28.7 %multiply_convert_fusion.10 = (bf16[1536,3072]{1,0:T(8,128)(2,1)S(1)}, bf16[1536,3072]{1,0:T(8,128)(2,1)}) fusion(f32[1536,3072]{1,0:T(8,128)} %get-tuple-element.936, f32[1536,3072]{1,0:T(8,128)} %fusion.200, f32[1536]{0:T(1024)S(1)} %add.582, f32[1536,3072]{1,0:T(8,128)} %get-tuple-element.940, f32[1536,3072]{1,0:T(8,128)} %fusion.202), kind=kLoop, calls=%fused_computation.59.clone.1.clone | loop fusion | flops 28311552 | bytes 94377984 | tf_op jit(solution)/shard_map/while/body/eval_jaxpr/while/body/eval_jaxpr/convert_element_type | solution.py:98
  1427.0 9.0 fusion.200
  1436.0 17.2 multiply_reduce_fusion.12
  1461.4 8.9 fusion.202
  1470.2 17.1 multiply_reduce_fusion.13
  1487.3 28.7 %multiply_convert_fusion.10 = (bf16[1536,3072]{1,0:T(8,128)(2,1)S(1)}, bf16[1536,3072]{1,0:T(8,128)(2,1)}) fusion(f32[1536,3072]{1,0:T(8,128)} %get-tuple-element.936, f32[1536,3072]{1,0:T(8,128)} %fusion.200, f32[1536]{0:T(1024)S(1)} %add.582, f32[1536,3072]{1,0:T(8,128)} %get-tuple-element.940, f32[1536,3072]{1,0:T(8,128)} %fusion.202), kind=kLoop, calls=%fused_computation.59.clone.1.clone | loop fusion | flops 28311552 | bytes 94377984 | tf_op jit(solution)/shard_map/while/body/eval_jaxpr/while/body/eval_jaxpr/convert_element_type | solution.py:98
  1557.4 23.5 %reduce-scatter.21.cloned.1.call-done = bf16[1536,320]{0,1:T(8,128)(2,1)} async-done(((bf16[6144,320]{0,1:T(8,128)(2,1)}), bf16[1536,320]{0,1:T(8,128)(2,1)}) %reduce-scatter.21.cloned.1.call-update) | async-done | bytes 983056 | tf_op jit(solution)/shard_map/reduce_scatter | solution.py:261
  1580.9 45.6 %reduce-scatter.23.cloned.1.call-done = bf16[1536,320]{0,1:T(8,128)(2,1)} async-done(((bf16[6144,320]{0,1:T(8,128)(2,1)}), bf16[1536,320]{0,1:T(8,128)(2,1)}) %reduce-scatter.23.cloned.1.call-update) | async-done | bytes 983056 | tf_op jit(solution)/shard_map/reduce_scatter | solution.py:264
  1626.5 8.7 convolution_convert_fusion
  1635.3 18.2 reduce-scatter.33.cloned.1.call-done
  1655.3 26.0 %reduce-scatter.31.cloned.1.call-done = bf16[320,320]{1,0:T(8,128)(2,1)} async-done(((bf16[1280,320]{1,0:T(8,128)(2,1)}), bf16[320,320]{1,0:T(8,128)(2,1)}) %reduce-scatter.31.cloned.1.call-update) | async-done | bytes 204816
  1683.2 25.2 %reduce-scatter.29.cloned.1.call-done = bf16[320,320]{1,0:T(8,128)(2,1)} async-done(((bf16[1280,320]{1,0:T(8,128)(2,1)}), bf16[320,320]{1,0:T(8,128)(2,1)}) %reduce-scatter.29.cloned.1.call-update) | async-done | bytes 204816 | tf_op jit(solution)/shard_map/reduce_scatter | solution.py:297
  1708.3 39.4 %reduce-scatter.27.cloned.1.call-done = bf16[320,3,320]{2,0,1:T(8,128)(2,1)} async-done(((bf16[1280,3,320]{2,0,1:T(8,128)(2,1)}), bf16[320,3,320]{2,0,1:T(8,128)(2,1)}) %reduce-scatter.27.cloned.1.call-update) | async-done | bytes 614416 | tf_op jit(solution)/shard_map/reduce_scatter | solution.py:291
  1747.8 8.6 convolution_bitcast_fusion
  1759.2 41.8 %all-reduce.5.cloned.1.call-done = (bf16[320,3,320]{2,0,1:T(8,128)(2,1)}, bf16[320,320]{1,0:T(8,128)(2,1)}, bf16[320,320]{1,0:T(8,128)(2,1)}, bf16[320,320]{1,0:T(8,128)(2,1)}) async-done(((bf16[320,3,320]{2,0,1:T(8,128)(2,1)}, bf16[320,320]{1,0:T(8,128)(2,1)}, bf16[320,320]{1,0:T(8,128)(2,1)}, bf16[320,320]{1,0:T(8,128)(2,1)}), (bf16[320,3,320]{2,0,1:T(8,128)(2,1)}, bf16[320,320]{1,0:T(8,128)(2,1)}, ...) | async-done | bytes 1228816 | tf_op jit(solution)/shard_map/psum | solution.py:305
  1808.6 130.8 %reduce-scatter.25.cloned.1.call-done = f32[1536,320]{0,1:T(8,128)} async-done(((f32[1536,1280]{0,1:T(8,128)}), f32[1536,320]{0,1:T(8,128)}) %reduce-scatter.25.cloned.1.call-update) | async-done | bytes 1966096 | tf_op jit(solution)/shard_map/reduce_scatter | solution.py:47
  1941.5 11.3 all-reduce.1
  1952.8 12.7 all-reduce
  (265 shorter events, 304.2 us)
Async XLA Ops:
  7.2 3.3 copy-start.2
  7.2 18.4 copy-start.21
  7.2 39.1 %all-gather.9.cloned.1.call-start = ((), (), s32[]{:S(2)}) async-start(), calls=%async_computation.11 | async-start | bytes 4915200 | tf_op jit(solution)/shard_map/all_gather | solution.py:133
  10.4 114.5 %all-gather.7.cloned.1.call-start = ((), (), s32[]{:S(2)}) async-start(), calls=%async_computation.10 | async-start | bytes 4915200 | tf_op jit(solution)/shard_map/all_gather | solution.py:35
  25.0 0.6 copy-start.18
  26.8 163.9 %all-gather.11.cloned.1.call-start = ((), (), s32[]{:S(2)}) async-start(), calls=%async_computation.12 | async-start | bytes 9830400 | tf_op jit(solution)/shard_map/all_gather | solution.py:145
  132.5 2.6 copy-start.13
  135.1 1.6 copy-start.17
  135.1 2.6 copy-start.30
  136.7 405.3 %reduce-scatter.15.cloned.1.call-start = ((), (), s32[]{:S(2)}) async-start(), calls=%async_computation.13 | async-start | bytes 9830400 | tf_op jit(solution)/shard_map/reduce_scatter | solution.py:39
  137.7 12.0 copy-start.26
  149.7 1.3 copy-start.6
  211.5 188.8 %copy-start.9 = (bf16[320,1280]{0,1:T(8,128)(2,1)S(1)}, bf16[320,1280]{0,1:T(8,128)(2,1)}, u32[]{:S(2)}) copy-start(bf16[320,1280]{0,1:T(8,128)(2,1)} %all_gather.30) | copy-start | bytes 2457604
  217.7 12.2 copy-start
  264.7 12.2 copy-start
  311.7 12.2 copy-start
  358.7 12.2 copy-start
  400.3 5.3 copy-start.10
  400.3 5.3 copy-start.24
  405.6 136.4 %copy-start.3 = (f32[1536,320]{0,1:T(8,128)S(1)}, f32[1536,320]{0,1:T(8,128)}, u32[]{:S(2)}) copy-start(f32[1536,320]{0,1:T(8,128)} %param.14) | copy-start | bytes 5898244
  405.6 229.8 %all-gather.13.cloned.1.call-start = ((), (), s32[]{:S(2)}) async-start(), calls=%async_computation.14 | async-start | bytes 4915200 | tf_op jit(solution)/shard_map/all_gather | solution.py:35
  545.2 15.3 copy-start.8
  560.4 152.0 %all-gather.15.cloned.1.call-start = ((), (), s32[]{:S(2)}) async-start(), calls=%async_computation.16 | async-start | bytes 4915200 | tf_op jit(solution)/shard_map/all_gather | solution.py:43
  561.5 296.7 %reduce-scatter.19.cloned.1.call-start = ((), (), s32[]{:S(2)}) async-start(), calls=%async_computation.17 | async-start | bytes 9830400 | tf_op jit(solution)/shard_map/reduce_scatter | solution.py:47
  584.0 128.5 %copy-start.14 = (bf16[320,1280]{0,1:T(8,128)(2,1)S(1)}, bf16[320,1280]{0,1:T(8,128)(2,1)}, u32[]{:S(2)}) copy-start(bf16[320,1280]{0,1:T(8,128)(2,1)} %all_gather.33) | copy-start | bytes 2457604
  717.1 1.0 copy-start.15
  723.3 274.2 %reduce-scatter.17.cloned.1.call-start = ((), (), s32[]{:S(2)}) async-start(), calls=%async_computation.15 | async-start | bytes 9830400 | tf_op jit(solution)/shard_map/reduce_scatter | solution.py:39
  731.1 127.1 %copy-start.5 = (f32[1536,320]{0,1:T(8,128)S(1)}, f32[1536,320]{0,1:T(8,128)}, u32[]{:S(2)}) copy-start(f32[1536,320]{0,1:T(8,128)} %get-tuple-element.700) | copy-start | bytes 5898244
  731.2 349.0 %all-gather.17.cloned.1.call-start = ((), (), s32[]{:S(2)}) async-start(), calls=%async_computation.18 | async-start | bytes 4915200 | tf_op jit(solution)/shard_map/all_gather | solution.py:43
  1003.2 577.8 %reduce-scatter.21.cloned.1.call-start = ((), (), s32[]{:S(2)}) async-start(), calls=%async_computation.19 | async-start | bytes 4915200 | tf_op jit(solution)/shard_map/reduce_scatter | solution.py:261
  1003.2 83.5 %copy-start.12 = (s32[6144]{0:T(1024)S(1)}, s32[6144]{0:T(1024)}, u32[]{:S(2)}) copy-start(s32[6144]{0:T(1024)} %get-tuple-element.1083) | copy-start | bytes 73732
  1003.2 83.5 %copy-start.25 = (s32[1536]{0:T(1024)S(1)}, s32[1536]{0:T(1024)}, u32[]{:S(2)}) copy-start(s32[1536]{0:T(1024)} %copy-done.24) | copy-start | bytes 18436
  1176.9 9.0 copy-start.1
  1289.9 9.0 copy-start.1
  1403.0 9.0 copy-start.1
  1516.0 9.0 copy-start.1
  1539.3 87.2 %reduce-scatter.23.cloned.1.call-start = ((), (), s32[]{:S(2)}) async-start(), calls=%async_computation.20 | async-start | bytes 4915200 | tf_op jit(solution)/shard_map/reduce_scatter | solution.py:264
  1540.1 6.0 copy-start.11
  1540.1 113.5 %reduce-scatter.33.cloned.1.call-start = ((), (), s32[]{:S(2)}) async-start(), calls=%async_computation.25 | async-start | bytes 1228800
  1545.9 5.6 copy-start.27
  1545.9 5.7 copy-start.16
  1546.0 135.4 %reduce-scatter.31.cloned.1.call-start = ((), (), s32[]{:S(2)}) async-start(), calls=%async_computation.24 | async-start | bytes 1228800
  1551.5 156.8 %reduce-scatter.29.cloned.1.call-start = ((), (), s32[]{:S(2)}) async-start(), calls=%async_computation.23 | async-start | bytes 1228800 | tf_op jit(solution)/shard_map/reduce_scatter | solution.py:297
  1551.7 5.6 copy-start.7
  1557.2 190.5 %reduce-scatter.27.cloned.1.call-start = ((), (), s32[]{:S(2)}) async-start(), calls=%async_computation.22 | async-start | bytes 3686400 | tf_op jit(solution)/shard_map/reduce_scatter | solution.py:291
  1635.2 112.5 %copy-start.28 = (bf16[1536,320]{0,1:T(8,128)(2,1)S(1)}, bf16[1536,320]{0,1:T(8,128)(2,1)}, u32[]{:S(2)}) copy-start(bf16[1536,320]{0,1:T(8,128)(2,1)} %reduce-scatter.21.cloned.1.call-done) | copy-start | bytes 2949124
  1635.2 112.5 %copy-start.29 = (bf16[1536,320]{0,1:T(8,128)(2,1)S(1)}, bf16[1536,320]{0,1:T(8,128)(2,1)}, u32[]{:S(2)}) copy-start(bf16[1536,320]{0,1:T(8,128)(2,1)} %reduce-scatter.23.cloned.1.call-done) | copy-start | bytes 2949124
  1635.3 165.8 %all-reduce.5.cloned.1.call-start = ((), (), s32[]{:S(2)}) async-start(), calls=%async_computation.26 | async-start | bytes 2949120 | tf_op jit(solution)/shard_map/psum | solution.py:305
  1747.7 191.7 %reduce-scatter.25.cloned.1.call-start = ((), (), s32[]{:S(2)}) async-start(), calls=%async_computation.21 | async-start | bytes 9830400 | tf_op jit(solution)/shard_map/reduce_scatter | solution.py:47
  1756.4 2.8 copy-start.31
  1756.4 183.0 %copy-start.4 = (f32[1536,320]{0,1:T(8,128)S(1)}, f32[1536,320]{0,1:T(8,128)}, u32[]{:S(2)}) copy-start(f32[1536,320]{0,1:T(8,128)} %param.14) | copy-start | bytes 5898244
  1756.5 183.0 %copy-start.19 = (f32[1536]{0:T(1024)S(1)}, f32[1536]{0:T(1024)}, u32[]{:S(2)}) copy-start(f32[1536]{0:T(1024)} %copy-done.18) | copy-start | bytes 18436
  1756.5 183.0 %copy-start.22 = (f32[320]{0:T(512)S(1)}, f32[320]{0:T(512)}, u32[]{:S(2)}) copy-start(f32[320]{0:T(512)} %param.16) | copy-start | bytes 3844
  1802.8 150.0 %copy-start.23 = (f32[320]{0:T(512)S(1)}, f32[320]{0:T(512)}, u32[]{:S(2)}) copy-start(f32[320]{0:T(512)} %get-tuple-element.642) | copy-start | bytes 3844
  1802.8 162.7 %copy-start.20 = (f32[1536]{0:T(1024)S(1)}, f32[1536]{0:T(1024)}, u32[]{:S(2)}) copy-start(f32[1536]{0:T(1024)} %get-tuple-element.721) | copy-start | bytes 18436
Sparse Core Ops, SparseCore 0:
  10.6 35.6 all-gather.8
  48.4 76.4 all-gather.6
  136.8 53.8 all-gather.10
  405.7 136.2 reduce-scatter.14
  560.5 74.8 all-gather.12
  637.4 74.9 all-gather.14
  723.4 134.7 reduce-scatter.18
  860.6 136.9 reduce-scatter.16
  1003.3 76.8 all-gather.16
  1539.4 41.4 reduce-scatter.20
  1583.6 42.8 reduce-scatter.22
  1629.0 24.5 reduce-scatter.32
  1656.9 24.4 reduce-scatter.30
  1683.8 24.4 reduce-scatter.28
  1710.9 36.7 reduce-scatter.26
  1751.1 49.8 all-reduce.4
  1803.2 136.2 reduce-scatter.24
where the time goes:
time: 1990 us; the launch traced here: 1980 us
  waiting for transfers between devices  1080 us (54%)
  matrix products  537 us (27%)
  other arithmetic  198 us (10%)
  blocking collectives  91.6 us (5%)
  local copies, waits for them, and re-layouts  55.7 us (3%)
    reduce_scatter x2, waiting for transfers between devices, branch_total(): return lax.psum_scatter(values, 'col', scatter_dimension=1, tiled=True)  261 us
    reduce_scatter x2, waiting for transfers between devices, grads_out(): return lax.psum_scatter(values, 'col', scatter_dimension=1, tiled=True)  258 us
    dot_general x16, matrix products, scores_for(): jnp.einsum('qd,kd->qk', queries, keys, preferred_element_type=jnp.float32)  205 us
    all_gather x2, waiting for transfers between devices, grads_in(): return lax.all_gather(values, 'col', axis=1, tiled=True)  149 us
    all_gather x2, waiting for transfers between devices, features(): return lax.all_gather(values, 'col', axis=1, tiled=True)  130 us
    convert_element_type x4, other arithmetic, block_terms(): (weight_piece * (slope_piece - deltas[:, None])).astype(jnp.bfloat16)  115 us
    dot_general x8, matrix products, forward_one_block(): jnp.dot(jnp.exp(scores[piece] - log_totals[:, None]).astype(jnp.bfloat16)...  72.6 us
    dot_general x8, matrix products, block_terms(): jnp.einsum('qd,kd->qk', block_go, head_v[lower:lower + LEN], preferred_el...  71.5 us
  transfers between devices with their start and end apart: 17, of which 17 were waited for; matrix products, arithmetic and copies ran while one was open for 4% of the time, Pallas kernels for 0%

commit v1 on v0

v1 whole, which is shorter than its diff:
```python
import functools
import math

import jax
import jax.numpy as jnp
from jax import lax
from jax.experimental import pallas as pl
from jax.experimental.pallas import tpu as pltpu
from jax.sharding import PartitionSpec as P

D = 1280
HD = 80
BLK = 256
LANES = 128

epsilon = 1e-06
scale_base = 1.442695041
excluded = -1e30

bf16 = jnp.bfloat16
f32 = jnp.float32


def dot(left, right):
    return jnp.dot(left, right, preferred_element_type=f32)


def product(form, left, right):
    return jnp.einsum(form, left, right, preferred_element_type=f32)


def three_terms(values):
    high = values.astype(bf16)
    rest = values - high.astype(f32)
    middle = rest.astype(bf16)
    return [high, middle, (rest - middle.astype(f32)).astype(bf16)]


def block_bias(starts_ref, first_block, width, block_count):
    shape = (block_count, width)
    block = lax.broadcasted_iota(jnp.int32, shape, 0)
    own = lax.broadcasted_iota(jnp.int32, shape, 1) // BLK
    start = jnp.zeros(shape, jnp.int32)
    for number in range(width // BLK):
        start = jnp.where(own == number, starts_ref[first_block + number], start)
    return jnp.where((block >= start) & (block <= first_block + own), 0.0, excluded).astype(bf16)


def extended(top, width, block_count, first_block, extra):
    row = lax.broadcasted_iota(jnp.int32, (LANES - HD, width), 0)
    block = first_block + lax.broadcasted_iota(jnp.int32, (LANES - HD, width), 1) // BLK
    marks = (row >= block_count) & (row < block_count + extra)
    if block_count:
        marks = marks | (row == block)
    return jnp.concatenate([top, jnp.where(marks, 1.0, 0.0).astype(bf16)], axis=0).T


def padded(parts, width):
    used = sum(part.shape[0] for part in parts)
    return jnp.concatenate(list(parts) + [jnp.zeros((LANES - used, width), bf16)], axis=0)


def forward_kernel(starts_ref, qkv_ref, out_ref, lse_ref, key_scr, *, tokens, part, tile):
    block_count = tokens // BLK
    per_part = part // tile
    per_tile = tile // BLK
    for number in range(tokens // tile):
        source, at = divmod(number, per_part)
        key_scr[number * tile : (number + 1) * tile, :] = extended(
            qkv_ref[source, HD : 2 * HD, at * tile : (at + 1) * tile],
            tile,
            block_count,
            number * per_tile,
            0,
        )

    def query_tile(number, carried):
        source = number // per_part
        at = pl.multiple_of((number % per_part) * tile, tile)
        bias = block_bias(starts_ref, number * per_tile, tile, block_count)
        query = padded([qkv_ref[source, 0:HD, pl.ds(at, tile)], bias], tile)

        def key_tile(key_number, state):
            largest, total, result = state
            keys = key_scr[pl.ds(pl.multiple_of(key_number * tile, tile), tile), :]
            scores = dot(keys, query)
            key_at = pl.multiple_of((key_number % per_part) * tile, tile)
            values = qkv_ref[key_number // per_part, 2 * HD : 3 * HD, pl.ds(key_at, tile)]
            newest = jnp.maximum(largest, jnp.max(scores, axis=0, keepdims=True))
            factor = jnp.exp(largest - newest)
            weights = jnp.exp(scores - newest)
            total = total * factor + jnp.sum(weights, axis=0, keepdims=True)
            result = result * factor + dot(values, weights.astype(bf16))
            return newest, total, result

        largest, total, result = lax.fori_loop(
            starts_ref[number * per_tile] // per_tile,
            number + 1,
            key_tile,
            (
                jnp.full((1, tile), -jnp.inf, f32),
                jnp.zeros((1, tile), f32),
                jnp.zeros((HD, tile), f32),
            ),
        )
        out_ref[source, :, pl.ds(at, tile)] = result / total
        lse_ref[source, :, pl.ds(at, tile)] = largest + jnp.log(total)
        return carried

    lax.fori_loop(0, tokens // tile, query_tile, 0)


def backward_kernel(
    starts_ref,
    scale_ref,
    qkv_ref,
    go_ref,
    out_ref,
    lse_ref,
    grad_ref,
    dim_ref,
    key_scr,
    value_scr,
    key_grad,
    value_grad,
    *,
    tokens,
    part,
    tile,
):
    block_count = tokens // BLK
    per_part = part // tile
    per_tile = tile // BLK
    for number in range(tokens // tile):
        source, at = divmod(number, per_part)
        columns = slice(at * tile, (at + 1) * tile)
        rows = slice(number * tile, (number + 1) * tile)
        key_scr[rows, :] = extended(
            qkv_ref[source, HD : 2 * HD, columns], tile, block_count, number * per_tile, 3
        )
        value_scr[rows, :] = extended(qkv_ref[source, 2 * HD : 3 * HD, columns], tile, 0, 0, 3)
    key_grad[...] = jnp.zeros_like(key_grad)
    value_grad[...] = jnp.zeros_like(value_grad)

    def query_tile(number, dim_total):
        source = number // per_part
        at = pl.multiple_of((number % per_part) * tile, tile)
        query_t = qkv_ref[source, 0:HD, pl.ds(at, tile)]
        go_t = go_ref[source, :, pl.ds(at, tile)]
        delta = jnp.sum(
            go_t.astype(f32) * out_ref[source, :, pl.ds(at, tile)], axis=0, keepdims=True
        )
        lse = lse_ref[source, :, pl.ds(at, tile)]
        bias = block_bias(starts_ref, number * per_tile, tile, block_count)
        query_ext = padded([query_t, bias] + three_terms(-lse), tile)
        go_ext = padded([go_t] + three_terms(-delta), tile)
        query = padded([query_t], tile).T
        go = padded([go_t], tile).T

        def key_tile(key_number, total):
            rows = pl.ds(pl.multiple_of(key_number * tile, tile), tile)
            key_at = pl.multiple_of((key_number % per_part) * tile, tile)
            keys_t = qkv_ref[key_number // per_part, HD : 2 * HD, pl.ds(key_at, tile)]
            weights = jnp.exp(dot(key_scr[rows, :], query_ext))
            slopes = (weights * dot(value_scr[rows, :], go_ext)).astype(bf16)
            value_grad[rows, :] += dot(weights.astype(bf16), go)
            key_grad[rows, :] += dot(slopes, query)
            return total + dot(keys_t, slopes)

        grad = lax.fori_loop(
            starts_ref[number * per_tile] // per_tile,
            number + 1,
            key_tile,
            jnp.zeros((HD, tile), f32),
        )
        grad_ref[source, 0:HD, pl.ds(at, tile)] = (grad * scale_ref[...]).astype(bf16)
        return dim_total + jnp.sum(grad * query_t.astype(f32), axis=1, keepdims=True)

    dim_ref[...] = lax.fori_loop(0, tokens // tile, query_tile, jnp.zeros((HD, 1), f32))
    for number in range(tokens // tile):
        source, at = divmod(number, per_part)
        columns = slice(at * tile, (at + 1) * tile)
        rows = slice(number * tile, (number + 1) * tile)
        grad_ref[source, HD : 2 * HD, columns] = key_grad[rows, :].T[:HD].astype(bf16)
        grad_ref[source, 2 * HD : 3 * HD, columns] = value_grad[rows, :].T[:HD].astype(bf16)


in_vmem = pl.BlockSpec(memory_space=pltpu.VMEM)
in_smem = pl.BlockSpec(memory_space=pltpu.SMEM)


def attend(starts, qkv, tile):
    parts, _, part = qkv.shape
    tokens = parts * part
    return pl.pallas_call(
        functools.partial(forward_kernel, tokens=tokens, part=part, tile=tile),
        out_shape=(
            jax.ShapeDtypeStruct((parts, HD, part), f32),
            jax.ShapeDtypeStruct((parts, 1, part), f32),
        ),
        in_specs=[in_smem, in_vmem],
        out_specs=(in_vmem, in_vmem),
        scratch_shapes=[pltpu.VMEM((tokens, LANES), bf16)],
        compiler_params=pltpu.CompilerParams(vmem_limit_bytes=50 << 20),
    )(starts, qkv)


def attend_back(starts, scale, qkv, go, out, lse, tile):
    parts, _, part = qkv.shape
    tokens = parts * part
    return pl.pallas_call(
        functools.partial(backward_kernel, tokens=tokens, part=part, tile=tile),
        out_shape=(
            jax.ShapeDtypeStruct((parts, 3 * HD, part), bf16),
            jax.ShapeDtypeStruct((HD, 1), f32),
        ),
        in_specs=[in_smem] + [in_vmem] * 5,
        out_specs=(in_vmem, in_vmem),
        scratch_shapes=[pltpu.VMEM((tokens, LANES), bf16)] * 2
        + [pltpu.VMEM((tokens, LANES), f32)] * 2,
        compiler_params=pltpu.CompilerParams(vmem_limit_bytes=58 << 20),
    )(starts, scale.reshape(HD, 1), qkv, go, out, lse)


def on_device(
    rows, cols, residual_in, seq_ids, norm1_gain, w_qkv, per_dim, w_out, norm2_gain, w_up, w_down, out_grad
):
    count, width = residual_in.shape
    heads = width // HD
    twins = rows // heads
    sub = count // cols
    share = w_qkv.shape[0]
    tile = 768 if count % 768 == 0 else BLK
    here = lax.axis_index("col")

    block_seq = seq_ids[::BLK]
    starts = jnp.sum((block_seq[None, :] < block_seq[:, None]).astype(jnp.int32), axis=1)

    qkv_local = w_qkv.astype(bf16).reshape(share, 3, heads, HD).transpose(0, 2, 1, 3)
    qkv_copy = lax.all_gather(
        qkv_local.reshape(share, heads * 3 * HD), "row", axis=0, tiled=True
    )
    stacked = jnp.stack([w_out.T, w_up, w_down.T], axis=0).astype(bf16)
    gathered = lax.all_gather(stacked, ("row", "col"), axis=0)
    gathered = (
        gathered.reshape(rows, cols, 3, share, width)
        .transpose(2, 0, 3, 1, 4)
        .reshape(3, rows * share, cols * width)
    )
    out_copy, up_copy, down_copy = gathered[0], gathered[1], gathered[2]
    gains = lax.all_gather(jnp.stack([norm1_gain, norm2_gain]), "col", axis=1, tiled=True)
    gain_one, gain_two = gains[0][:, None], gains[1][:, None]

    residual = residual_in.T
    totals = lax.psum(jnp.sum(residual * residual, axis=0), "col")
    inverse_one = lax.rsqrt(totals / D + epsilon)[None, :]
    normed = (residual * inverse_one * norm1_gain[:, None]).astype(bf16)
    normed_all = lax.all_gather(normed, "col", axis=0, tiled=True)
    projected = product("dj,dn->jn", qkv_copy, normed_all).reshape(heads, 3, HD, count)
    scale = jax.nn.softplus(per_dim) * scale_base / math.sqrt(HD)
    factors = jnp.stack([scale, jnp.ones_like(scale), jnp.ones_like(scale)])
    qkv = (projected * factors[None, :, :, None]).astype(bf16).reshape(heads, 3 * HD, count)
    qkv_heads = lax.all_to_all(jnp.repeat(qkv, twins, axis=0), "row", 0, 0, tiled=True)

    result, lse = attend(starts, qkv_heads, tile)
    leaving = result.astype(bf16).reshape(rows, HD, cols, sub).transpose(0, 2, 1, 3)
    arrived = lax.all_to_all(leaving.reshape(rows * cols, HD, sub), ("row", "col"), 0, 0, tiled=True)
    attended = (
        arrived.reshape(rows, cols, HD, sub)[::twins].transpose(1, 0, 2, 3).reshape(D, sub)
    )

    def spread(values):
        pieces = values.reshape(width, cols, sub).transpose(1, 0, 2)
        return lax.all_to_all(pieces, "col", 0, 0, tiled=True).reshape(cols * width, sub)

    def collect(values):
        pieces = lax.all_to_all(values.reshape(cols, width, sub), "col", 0, 0, tiled=True)
        return pieces.transpose(1, 0, 2).reshape(width, count)

    grad_mlp = spread(out_grad.T.astype(bf16))
    own_inverse = lax.dynamic_slice_in_dim(inverse_one, here * sub, sub, 1)
    own_normed = lax.dynamic_slice_in_dim(normed_all, here * sub, sub, 1)
    branch = product("dc,cn->dn", out_copy, attended)
    middle = own_normed.astype(f32) / (own_inverse * gain_one) + branch
    inverse_two = lax.rsqrt(jnp.sum(middle * middle, axis=0, keepdims=True) / D + epsilon)
    normed_two = (middle * inverse_two * gain_two).astype(bf16)
    up_proj = product("df,dn->fn", up_copy, normed_two)
    sigmoid_up = jax.nn.sigmoid(up_proj)
    activated = (up_proj * sigmoid_up).astype(bf16)
    change = branch + product("df,fn->dn", down_copy, activated)
    grad_act = product("df,dn->fn", down_copy, grad_mlp)
    grad_up = (grad_act * sigmoid_up * (1.0 + up_proj * (1.0 - sigmoid_up))).astype(bf16)
    grad_two = product("df,fn->dn", up_copy, grad_up)
    along = jnp.sum(gain_two * grad_two * middle, axis=0, keepdims=True)
    back_two = inverse_two * gain_two * grad_two - middle * inverse_two**3 * along / D
    gain_two_part = jnp.sum(grad_two * middle * inverse_two, axis=1)
    grad_branch = (grad_mlp.astype(f32) + back_two).astype(bf16)
    grad_attended = product("dc,dn->cn", out_copy, grad_branch).astype(bf16)

    leaving = grad_attended.reshape(cols, heads, HD, sub).transpose(1, 0, 2, 3)
    leaving = jnp.repeat(leaving, twins, axis=0).reshape(rows * cols, HD, sub)
    arrived = lax.all_to_all(leaving, ("row", "col"), 0, 0, tiled=True)
    go = arrived.reshape(rows, cols, HD, sub).transpose(0, 2, 1, 3).reshape(rows, HD, count)

    output = residual_in + collect(change.astype(bf16)).astype(f32).T
    back_two_here = collect(back_two.astype(bf16)).astype(f32)

    parts = jnp.stack(
        [
            product("dn,cn->dc", grad_branch, attended),
            product("dn,fn->df", normed_two, grad_up),
            product("dn,fn->df", grad_mlp, activated),
        ]
    ).astype(bf16)
    parts = parts.reshape(3, rows, share, cols, width).transpose(1, 3, 0, 2, 4)
    parts = parts.reshape(rows * cols * 3, share, width)
    shard = lax.psum_scatter(parts, ("row", "col"), scatter_dimension=0, tiled=True)
    shard = lax.psum(shard, "dp").astype(f32)

    grad_heads, dim_part = attend_back(starts, scale, qkv_heads, go, result, lse, tile)
    grad_projected = lax.all_to_all(grad_heads, "row", 0, 0, tiled=True)[::twins]

    grad_flat = grad_projected.reshape(heads * 3 * HD, count)
    grad_one_part = product("dj,jn->dn", qkv_copy, grad_flat)
    grad_one = lax.psum_scatter(
        grad_one_part.astype(bf16), "col", scatter_dimension=0, tiled=True
    ).astype(f32)
    qkv_part = product("dn,jn->dj", normed_all, grad_flat)
    own_head = (lax.axis_index("row") % twins == 0).astype(f32)
    gain_one_part = jnp.sum(qkv_part * qkv_copy.astype(f32), axis=1)
    small = jnp.concatenate([gain_one_part, gain_two_part, dim_part[:, 0] * own_head])
    small = lax.psum(small, ("dp", "row", "col"))
    gain_one_grad = lax.dynamic_slice_in_dim(small[:D], here * width, width) / norm1_gain
    gain_two_grad = lax.dynamic_slice_in_dim(small[D : 2 * D], here * width, width)
    scale_grad = small[2 * D :] / scale * (scale_base / math.sqrt(HD)) * jax.nn.sigmoid(per_dim)
    qkv_shard = lax.psum_scatter(qkv_part.astype(bf16), "row", scatter_dimension=0, tiled=True)
    qkv_grad = lax.psum(qkv_shard, "dp").astype(f32)
    qkv_grad = qkv_grad.reshape(share, heads, 3, HD).transpose(0, 2, 1, 3).reshape(share, 3, width)

    along_one = lax.psum(jnp.sum(normed_all.astype(f32) * grad_one_part, axis=0), "col")
    back_one = inverse_one * norm1_gain[:, None] * grad_one - residual * inverse_one**2 * (
        along_one / D
    )
    input_grad = out_grad + (back_two_here + back_one).T
    return (
        output,
        input_grad,
        gain_one_grad,
        qkv_grad,
        scale_grad,
        shard[0].T,
        gain_two_grad,
        shard[1],
        shard[2].T,
    )


def solution(mesh):
    in_specs = (
        P(("dp", "row"), "col"),
        P("dp"),
        P("col"),
        P("row", None, "col"),
        P(),
        P("col", "row"),
        P("col"),
        P("row", "col"),
        P("col", "row"),
        P(("dp", "row"), "col"),
    )
    out_specs = (
        P(("dp", "row"), "col"),
        P(("dp", "row"), "col"),
        P("col"),
        P("row", None, "col"),
        P(),
        P("col", "row"),
        P("col"),
        P("row", "col"),
        P("col", "row"),
    )
    return jax.shard_map(
        functools.partial(on_device, mesh.shape["row"], mesh.shape["col"]),
        mesh=mesh,
        in_specs=in_specs,
        out_specs=out_specs,
        check_vma=False,
    )
```

time: 1990 us -> 815 us (0.41)
  waiting for transfers between devices: 1080 us -> 375 us
  matrix products: 537 us -> 58.7 us
  other arithmetic: 198 us -> 19.5 us
  Pallas kernels: 0 us -> 75 us
  local copies, waits for them, and re-layouts: 55.7 us -> 112 us
  starting transfers between devices: 0.7 us -> 30.9 us
  blocking collectives: 91.6 us -> 119 us
    reduce_scatter x8 -> x2, waiting for transfers between devices: 653 us -> 73.7 us  [the longest x1 73.7 us: on_device(): lax.psum_scatter(grad_one_part.astype(bf16), 'col', scatter_dimension=0,...]
    dot_general x68 -> x12, matrix products: 537 us -> 58.7 us  [product(): return jnp.einsum(form, left, right, preferred_element_type=f32)]
    all_gather x6 -> x3, waiting for transfers between devices: 337 us -> 89.1 us  [the longest x1 78.6 us: on_device(): normed_all = lax.all_gather(normed, 'col', axis=0, tiled=True)]
    all_to_all x0 -> x7, waiting for transfers between devices: none -> 165 us  [the longest x2 66.2 us: collect(): lax.all_to_all(values.reshape(cols, width, sub), 'col', 0, 0, tiled=True)]
    convert_element_type x14 -> x6, other arithmetic: 136 us -> 5.51 us  [the longest x1 2.44 us: on_device(): (projected * factors[None, :, :, None]).astype(bf16)]
    pallas_call x0 -> x2, Pallas kernels: none -> 75 us  [the longest x1 46.1 us: attend_back(): pl.pallas_call(functools.partial(backward_kernel, tokens=tokens, part=par...]
    reduce_sum x9 -> x2, other arithmetic: 47.5 us -> 0.35 us  [the longest x1 0.18 us: on_device(): jnp.sum((block_seq[None, :] < block_seq[:, None]).astype(jnp.int32), axis=1)]
    unnamed x19 -> x8, waiting for transfers between devices: 45.2 us -> 0.12 us
  transfers between devices with their start and end apart: 17 -> 14, of which waited for: 17 -> 9; matrix products, arithmetic and copies ran while one was open for 4% -> 18% of each run, Pallas kernels for 0% -> 4%
where the time goes in v1:
time: 815 us; the launch traced here: 806 us
  waiting for transfers between devices  375 us (46%)
  blocking collectives  119 us (15%)
  local copies, waits for them, and re-layouts  112 us (14%)
  Pallas kernels  75 us (9%)
  matrix products  58.7 us (7%)
  starting transfers between devices  30.9 us (4%)
  other arithmetic  19.5 us (2%)
  between operations  14.9 us (2%)
    all_gather x1, waiting for transfers between devices, on_device(): normed_all = lax.all_gather(normed, 'col', axis=0, tiled=True)  78.6 us
    reduce_scatter x1, waiting for transfers between devices, on_device(): lax.psum_scatter(grad_one_part.astype(bf16), 'col', scatter_dimension=0,...  73.7 us
    all_to_all x2, waiting for transfers between devices, collect(): lax.all_to_all(values.reshape(cols, width, sub), 'col', 0, 0, tiled=True)  66.2 us
    psum x1, blocking collectives, on_device(): small = lax.psum(small, ('dp', 'row', 'col'))  61.5 us
    dot_general x12, matrix products, product(): return jnp.einsum(form, left, right, preferred_element_type=f32)  58.7 us
    psum x1, waiting for transfers between devices, on_device(): qkv_grad = lax.psum(qkv_shard, 'dp').astype(f32)  46.9 us
    pallas_call x1, Pallas kernels, attend_back(): pl.pallas_call(functools.partial(backward_kernel, tokens=tokens, part=par...  46.1 us
    all_to_all x1, waiting for transfers between devices, on_device(): lax.all_to_all(jnp.repeat(qkv, twins, axis=0), 'row', 0, 0, tiled=True)  43.8 us
  transfers between devices with their start and end apart: 14, of which 9 were waited for; matrix products, arithmetic and copies ran while one was open for 18% of the time, Pallas kernels for 4%

profile of v1, /device:TPU:0, one launch (start us, length us, event | category | flops | bytes accessed | tf_op | source)
XLA Modules:
  0.0 805.7 jit_solution(12901891955047811149)
XLA Ops:
  7.2 1.7 copy.92
  9.1 1.1 copy.94
  10.9 13.7 %psum.35 = f32[1536]{0:T(1024)S(1)} all-reduce(f32[1536]{0:T(1024)S(1)} %multiply_reduce_fusion.5), channel_id=1, replica_groups=mesh['dp'=2,'row'=4,'col'=4] {'col'}, use_global_device_ids=true, to_apply=%region_2.0 | all-reduce | flops 1536 | bytes 12288 | tf_op jit(solution)/shard_map/psum | solution.py:255
  24.7 1.2 fusion.5
  28.1 10.5 %all-gather.9.cloned.1.call-done = bf16[1280,960]{1,0:T(8,128)(2,1)} async-done(((bf16[320,960]{1,0:T(8,128)(2,1)}), bf16[1280,960]{1,0:T(8,128)(2,1)}) %all-gather.9.cloned.1.call-update) | async-done | bytes 2457616 | tf_op jit(solution)/shard_map/all_gather | solution.py:240
  38.6 78.6 %all-gather.7.cloned.1.call-done = bf16[1280,1536]{1,0:T(8,128)(2,1)} async-done(((bf16[320,1536]{1,0:T(8,128)(2,1)}), bf16[1280,1536]{1,0:T(8,128)(2,1)}) %all-gather.7.cloned.1.call-update) | async-done | bytes 3932176 | tf_op jit(solution)/shard_map/all_gather | solution.py:258
  117.2 7.1 fusion.14
  124.4 2.4 multiply_convert_fusion
  126.8 4.6 all-to-all-start
  132.5 43.8 %all-to-all-done.qkv_ref = bf16[4,240,1536]{2,1,0:T(8,128)(2,1)} async-done(((bf16[4,240,1536]{2,1,0:T(8,128)(2,1)}), bf16[4,240,1536]{2,1,0:T(8,128)(2,1)}, u32[]{:S(2)}, u32[]{:S(2)}) %all-to-all-start) | async-done | bytes 2949152 | tf_op jit(solution)/shard_map/all_to_all | solution.py:263
  176.3 28.9 %shard_map.169 = (f32[4,80,1536]{2,1,0:T(8,128)S(1)}, f32[4,1,1536]{2,1,0:T(1,128)S(1)}) custom-call(s32[24]{0:T(128)S(1)} %convert_reduce_fusion.starts_ref, bf16[4,240,1536]{2,1,0:T(8,128)(2,1)} %all-to-all-done.qkv_ref), custom_call_target="tpu_custom_call" | custom-call | tf_op jit(solution)/shard_map/pallas_call | solution.py:195
  205.4 1.1 copy-done
  206.5 1.0 pad_maximum_fusion
  207.6 4.8 all-to-all-start.1
  212.6 1.0 copy.124
  213.6 33.2 %all-gather = f32[4,320,2]{1,2,0:T(2,128)S(1)} all-gather(f32[1,320,2]{1,2,0:T(2,128)S(1)} %maximum_bitcast_fusion.1), channel_id=1, replica_groups=mesh['dp'=2,'row'=4,'col'=4] {'col'}, dimensions={0}, use_global_device_ids=true | all-gather | bytes 12800 | tf_op jit(solution)/shard_map/all_gather | solution.py:251
  248.0 4.0 all-to-all-start.3
  252.0 2.2 copy.95
  254.3 15.2 %copy.123 = bf16[4,4,3,320,320]{4,1,3,0,2:T(4,128)(2,1)S(1)} copy(bf16[4,4,3,320,320]{4,3,2,1,0:T(8,128)(2,1)} %bitcast.138) | data formatting | bytes 19660800 | tf_op jit(solution)/shard_map/reshape | solution.py:246
  269.5 5.7 fusion.10
  275.2 7.6 squeeze.21
  282.8 7.6 squeeze.23
  290.5 7.6 squeeze.22
  298.1 5.9 multiply_reduce_fusion.4
  304.0 3.3 fusion.9
  307.3 4.9 fusion.3
  312.2 2.1 multiply_reduce_fusion.2
  314.4 1.6 add_convert_fusion
  316.7 1.9 convolution_convert_fusion.2
  319.6 5.4 all-to-all-start.5
  325.8 24.8 %all-to-all-done.5 = bf16[16,80,384]{2,1,0:T(8,128)(2,1)S(1)} async-done(((bf16[16,80,384]{2,1,0:T(8,128)(2,1)}), bf16[16,80,384]{2,1,0:T(8,128)(2,1)S(1)}, u32[]{:S(2)}, u32[]{:S(2)}) %all-to-all-start.5) | async-done | bytes 983072 | tf_op jit(solution)/shard_map/all_to_all | solution.py:302
  350.6 1.1 copy.120
  351.6 46.1 %shard_map.170 = (bf16[4,240,1536]{2,1,0:T(8,128)(2,1)}, f32[80,1]{1,0:T(8,128)}) custom-call(s32[24]{0:T(128)} %copy-done.2, f32[80,1]{1,0:T(8,128)} %copy.102.scale_ref, bf16[4,240,1536]{2,1,0:T(8,128)(2,1)} %all-to-all-done.qkv_ref, bf16[4,80,1536]{2,1,0:T(8,128)(2,1)} %bitcast.147, f32[4,80,1536]{2,1,0:T(8,128)} %copy-done, f32[4,1,1536]{2,1,0:T(1,128)} %copy-done.1), custom_call_target="tpu_custom_call" | custom-call | tf_op jit(solution)/shard_map/pallas_call | solution.py:211
  397.7 4.6 all-to-all-start.6
  402.4 4.4 copy.103
  406.8 30.5 %all-to-all-done.6 = bf16[4,240,1536]{2,1,0:T(8,128)(2,1)} async-done(((bf16[4,240,1536]{2,1,0:T(8,128)(2,1)}), bf16[4,240,1536]{2,1,0:T(8,128)(2,1)}, u32[]{:S(2)}, u32[]{:S(2)}) %all-to-all-start.6) | async-done | bytes 2949152 | tf_op jit(solution)/shard_map/all_to_all | solution.py:321
  437.2 9.2 %fusion.11 = (bf16[1280,960]{0,1:T(8,128)(2,1)}, f32[1280]{0:T(1024)S(1)}) fusion(bf16[1280,960]{0,1:T(8,128)(2,1)} %copy.103, bf16[1280,1536]{1,0:T(8,128)(2,1)} %all-gather.7.cloned.1.call-done, bf16[960,1536]{1,0:T(8,128)(2,1)} %bitcast.35), kind=kOutput, calls=%fused_computation.61 | convolution fusion | flops 3779787520 | bytes 11801600 | tf_op jit(solution)/shard_map/dn,jn->dj/dot_general | solution.py:29
  446.4 4.5 copy.115
  450.9 1.5 copy-done.25
  452.4 3.7 fusion
  456.1 9.0 %reshape.216 = bf16[1,4,320,4,320]{2,1,4,3,0:T(4,128)(2,1)} reshape(bf16[1280,1280]{0,1:T(8,128)(2,1)} %fusion) | data formatting | bytes 6553600 | tf_op jit(solution)/shard_map/stack | solution.py:308
  465.1 8.0 copy.107
  473.1 3.7 convolution_convert_fusion.1
  476.8 5.3 stack.47
  482.1 2.9 copy.106
  485.0 2.2 convert_bitcast_fusion
  487.3 3.9 maximum_bitcast_fusion
  491.2 5.2 copy.108
  496.5 1.7 copy-done.12
  498.2 8.1 %multiply_reduce_fusion = (f32[1536]{0:T(1024)S(1)}, bf16[1280,1536]{1,0:T(8,128)(2,1)}) fusion(bf16[1280,1536]{1,0:T(8,128)(2,1)} %all-gather.7.cloned.1.call-done, bf16[1280,960]{1,0:T(8,128)(2,1)S(1)} %copy-done.12, bf16[960,1536]{1,0:T(8,128)(2,1)} %bitcast.35), kind=kOutput, calls=%fused_computation.3 | convolution fusion | flops 3782736384 | bytes 13277184 | tf_op jit(solution)/shard_map/dj,jn->dn/dot_general | solution.py:29
  506.3 3.5 all-to-all-start.4
  509.9 6.5 fusion.2
  516.4 17.9 %all-to-all-done.4 = bf16[4,320,384]{2,1,0:T(8,128)(2,1)S(1)} async-done(((bf16[4,320,384]{2,1,0:T(8,128)(2,1)}), bf16[4,320,384]{2,1,0:T(8,128)(2,1)S(1)}, u32[]{:S(2)}, u32[]{:S(2)}) %all-to-all-start.4) | async-done | bytes 983072 | tf_op jit(solution)/shard_map/all_to_all | solution.py:277
  534.3 3.5 all-to-all-start.2
  538.0 1.5 copy.119
  539.6 48.2 %all-to-all-done.2 = bf16[4,320,384]{2,1,0:T(8,128)(2,1)S(1)} async-done(((bf16[4,320,384]{2,1,0:T(8,128)(2,1)}), bf16[4,320,384]{2,1,0:T(8,128)(2,1)S(1)}, u32[]{:S(2)}, u32[]{:S(2)}) %all-to-all-start.2) | async-done | bytes 983072 | tf_op jit(solution)/shard_map/all_to_all | solution.py:277
  588.0 1.5 copy.118
  589.6 61.5 %psum.37 = f32[2640]{0:T(1024)S(1)} all-reduce(f32[2640]{0:T(1024)S(1)} %pad_maximum_fusion.2), channel_id=1, replica_groups=mesh['dp'=2,'row'=4,'col'=4] {'dp','row','col'}, use_global_device_ids=true, to_apply=%region_10.11 | all-reduce | flops 2640 | bytes 21120 | tf_op jit(solution)/shard_map/psum | solution.py:332
  651.8 10.9 %psum.36 = f32[1536]{0:T(1024)S(1)} all-reduce(f32[1536]{0:T(1024)S(1)} %get-tuple-element.64), channel_id=1, replica_groups=mesh['dp'=2,'row'=4,'col'=4] {'col'}, use_global_device_ids=true, to_apply=%region_7.8 | all-reduce | flops 1536 | bytes 12288 | tf_op jit(solution)/shard_map/psum | solution.py:340
  663.3 1.6 copy.116
  666.5 73.7 %reduce-scatter.6.cloned.1.call-done = bf16[320,1536]{1,0:T(8,128)(2,1)} async-done(((bf16[1280,1536]{1,0:T(8,128)(2,1)}), bf16[320,1536]{1,0:T(8,128)(2,1)}) %reduce-scatter.6.cloned.1.call-update) | async-done | bytes 983056 | tf_op jit(solution)/shard_map/reduce_scatter | solution.py:325
  740.2 6.0 bitcast_add_fusion
  746.1 46.9 %all-reduce.4.cloned.1.call-done = (bf16[320,3,320]{0,2,1:T(8,128)(2,1)}, bf16[3,320,320]{2,1,0:T(8,128)(2,1)}) async-done(((bf16[320,3,320]{0,2,1:T(8,128)(2,1)}, bf16[3,320,320]{2,1,0:T(8,128)(2,1)}), (bf16[320,3,320]{0,2,1:T(8,128)(2,1)}, bf16[3,320,320]{2,1,0:T(8,128)(2,1)})) %all-reduce.4.cloned.1.call-update) | async-done | bytes 1228816 | tf_op jit(solution)/shard_map/psum | solution.py:337
  793.0 2.6 copy.109
  (108 shorter events, 14.4 us)
Async XLA Ops:
  7.2 31.4 %all-gather.9.cloned.1.call-start = ((), (), s32[]{:S(2)}) async-start(), calls=%async_computation.12 | async-start | bytes 3276800 | tf_op jit(solution)/shard_map/all_gather | solution.py:240
  9.0 1.8 copy-start.3
  9.1 15.6 %copy-start.22 = (f32[320]{0:T(512)S(1)}, f32[320]{0:T(512)}, u32[]{:S(2)}) copy-start(f32[320]{0:T(512)} %param.12) | copy-start | bytes 3844
  10.2 107.0 %all-gather.7.cloned.1.call-start = ((), (), s32[]{:S(2)}) async-start(), calls=%async_computation.11 | async-start | bytes 4915200 | tf_op jit(solution)/shard_map/all_gather | solution.py:258
  24.7 1.3 copy-start.18
  24.7 1.5 copy-start.19
  25.9 1.0 copy-start.20
  25.9 228.4 %all-gather.5.cloned.1.call-start = ((), (), s32[]{:S(2)}) async-start(), calls=%async_computation.10 | async-start | bytes 12533760 | tf_op jit(solution)/shard_map/all_gather | solution.py:244
  26.1 1.8 copy-start.24
  126.8 49.5 %all-to-all-start = ((bf16[4,240,1536]{2,1,0:T(8,128)(2,1)}), bf16[4,240,1536]{2,1,0:T(8,128)(2,1)}, u32[]{:S(2)}, u32[]{:S(2)}) async-start(bf16[4,240,1536]{2,1,0:T(8,128)(2,1)} %multiply_convert_fusion), calls=%async_computation | async-start | bytes 5898240 | tf_op jit(solution)/shard_map/all_to_all | solution.py:263
  132.5 72.9 %copy-start.2 = (s32[24]{0:T(128)}, s32[24]{0:T(128)S(1)}, u32[]{:S(2)}) copy-start(s32[24]{0:T(128)S(1)} %convert_reduce_fusion.starts_ref) | copy-start | bytes 292
  205.2 1.3 copy-start
  205.2 1.3 copy-start.1
  206.5 5.9 copy-start.6
  207.6 39.4 %all-to-all-start.1 = ((bf16[16,80,384]{2,1,0:T(8,128)(2,1)}), bf16[16,80,384]{2,1,0:T(8,128)(2,1)S(1)}, u32[]{:S(2)}, u32[]{:S(2)}) async-start(bf16[16,80,384]{2,1,0:T(8,128)(2,1)} %bitcast.145), calls=%async_computation.1 | async-start | bytes 1966080 | tf_op jit(solution)/shard_map/all_to_all | solution.py:267
  212.4 1.2 copy-start.23
  247.0 0.9 copy-start.8
  248.0 59.3 %all-to-all-start.3 = ((bf16[4,320,384]{2,1,0:T(8,128)(2,1)}), bf16[4,320,384]{2,1,0:T(8,128)(2,1)S(1)}, u32[]{:S(2)}, u32[]{:S(2)}) async-start(bf16[4,320,384]{2,1,0:T(8,128)(2,1)} %bitcast.135), calls=%async_computation.3 | async-start | bytes 1966080 | tf_op jit(solution)/shard_map/all_to_all | solution.py:274
  298.1 5.9 copy-start.10
  303.9 10.4 %copy-start.7 = (f32[1280,384]{1,0:T(8,128)}, f32[1280,384]{1,0:T(8,128)S(1)}, u32[]{:S(2)}) copy-start(f32[1280,384]{1,0:T(8,128)S(1)} %get-tuple-element.60) | copy-start | bytes 5898244
  307.3 5.0 copy-start.11
  312.2 2.1 copy-start.14
  314.4 2.3 copy-start.9
  316.0 2.6 copy-start.15
  319.6 31.0 %all-to-all-start.5 = ((bf16[16,80,384]{2,1,0:T(8,128)(2,1)}), bf16[16,80,384]{2,1,0:T(8,128)(2,1)S(1)}, u32[]{:S(2)}, u32[]{:S(2)}) async-start(bf16[16,80,384]{2,1,0:T(8,128)(2,1)} %bitcast.32), calls=%async_computation.5 | async-start | bytes 1966080 | tf_op jit(solution)/shard_map/all_to_all | solution.py:302
  397.7 39.5 %all-to-all-start.6 = ((bf16[4,240,1536]{2,1,0:T(8,128)(2,1)}), bf16[4,240,1536]{2,1,0:T(8,128)(2,1)}, u32[]{:S(2)}, u32[]{:S(2)}) async-start(bf16[4,240,1536]{2,1,0:T(8,128)(2,1)} %get-tuple-element.15), calls=%async_computation.6 | async-start | bytes 5898240 | tf_op jit(solution)/shard_map/all_to_all | solution.py:321
  402.3 260.9 %reduce-scatter.10.cloned.1.call-start = ((), (), s32[]{:S(2)}) async-start(), calls=%async_computation.15 | async-start | bytes 3276800
  450.9 1.5 copy-start.25
  450.9 214.9 %reduce-scatter.8.cloned.1.call-start = ((), (), s32[]{:S(2)}) async-start(), calls=%async_computation.14 | async-start | bytes 12533760 | tf_op jit(solution)/shard_map/reduce_scatter | solution.py:317
  482.1 2.9 copy-start.13
  482.1 2.9 copy-start.16
  485.0 2.3 copy-start.5
  496.5 1.7 copy-start.12
  496.5 243.7 %reduce-scatter.6.cloned.1.call-start = ((), (), s32[]{:S(2)}) async-start(), calls=%async_computation.13 | async-start | bytes 4915200 | tf_op jit(solution)/shard_map/reduce_scatter | solution.py:325
  506.3 28.0 %all-to-all-start.4 = ((bf16[4,320,384]{2,1,0:T(8,128)(2,1)}), bf16[4,320,384]{2,1,0:T(8,128)(2,1)S(1)}, u32[]{:S(2)}, u32[]{:S(2)}) async-start(bf16[4,320,384]{2,1,0:T(8,128)(2,1)} %bitcast.27), calls=%async_computation.4 | async-start | bytes 1966080 | tf_op jit(solution)/shard_map/all_to_all | solution.py:277
  534.3 53.5 %all-to-all-start.2 = ((bf16[4,320,384]{2,1,0:T(8,128)(2,1)}), bf16[4,320,384]{2,1,0:T(8,128)(2,1)S(1)}, u32[]{:S(2)}, u32[]{:S(2)}) async-start(bf16[4,320,384]{2,1,0:T(8,128)(2,1)} %bitcast.21), calls=%async_computation.2 | async-start | bytes 1966080 | tf_op jit(solution)/shard_map/all_to_all | solution.py:277
  537.8 255.2 %all-reduce.4.cloned.1.call-start = ((), (), s32[]{:S(2)}) async-start(), calls=%async_computation.16 | async-start | bytes 2949120 | tf_op jit(solution)/shard_map/psum | solution.py:337
  587.9 1.5 copy-start.21
  663.3 76.9 %copy-start.4 = (f32[1536,320]{0,1:T(8,128)S(1)}, f32[1536,320]{0,1:T(8,128)}, u32[]{:S(2)}) copy-start(f32[1536,320]{0,1:T(8,128)} %param.10) | copy-start | bytes 5898244
  793.0 2.6 copy-start.17
Sparse Core Ops, SparseCore 0:
  10.3 28.2 all-gather.8
  40.8 76.4 all-gather.6
  120.1 110.1 all-gather.4
  451.0 44.7 reduce-scatter.9
  500.4 165.0 reduce-scatter.7
  667.6 72.4 reduce-scatter.5
  743.1 49.8 all-reduce.3

commit v2 on v1

v2 whole, which is shorter than its diff:
```python
import functools
import math

import jax
import jax.numpy as jnp
from jax import lax
from jax.experimental import pallas as pl
from jax.experimental.pallas import tpu as pltpu
from jax.sharding import PartitionSpec as P

D = 1280
HD = 80
BLK = 256
LANES = 128

epsilon = 1e-06
scale_base = 1.442695041
excluded = -1e30

bf16 = jnp.bfloat16
f32 = jnp.float32


def dot(left, right):
    return jnp.dot(left, right, preferred_element_type=f32)


def product(form, left, right):
    return jnp.einsum(form, left, right, preferred_element_type=f32)


def three_terms(values):
    high = values.astype(bf16)
    rest = values - high.astype(f32)
    middle = rest.astype(bf16)
    return [high, middle, (rest - middle.astype(f32)).astype(bf16)]


def block_bias(starts_ref, first_block, width, block_count):
    shape = (block_count, width)
    block = lax.broadcasted_iota(jnp.int32, shape, 0)
    own = lax.broadcasted_iota(jnp.int32, shape, 1) // BLK
    start = jnp.zeros(shape, jnp.int32)
    for number in range(width // BLK):
        start = jnp.where(own == number, starts_ref[first_block + number], start)
    return jnp.where((block >= start) & (block <= first_block + own), 0.0, excluded).astype(bf16)


def extended(top, width, block_count, first_block, extra):
    row = lax.broadcasted_iota(jnp.int32, (LANES - HD, width), 0)
    block = first_block + lax.broadcasted_iota(jnp.int32, (LANES - HD, width), 1) // BLK
    marks = (row >= block_count) & (row < block_count + extra)
    if block_count:
        marks = marks | (row == block)
    return jnp.concatenate([top, jnp.where(marks, 1.0, 0.0).astype(bf16)], axis=0).T


def padded(parts, width):
    used = sum(part.shape[0] for part in parts)
    return jnp.concatenate(list(parts) + [jnp.zeros((LANES - used, width), bf16)], axis=0)


def forward_kernel(starts_ref, place_ref, *refs, tokens, part, tile, rows):
    pieces = refs[: -4]
    out_ref, lse_ref, qkv_ref, key_scr = refs[-4:]
    half = pieces[0].shape[1]
    for number, piece in enumerate(pieces):
        flip, at = number % rows, number // rows
        qkv_ref[jnp.bitwise_xor(place_ref[0], flip), :, at * half : (at + 1) * half] = piece[...]
    block_count = tokens // BLK
    per_part = part // tile
    per_tile = tile // BLK
    for number in range(tokens // tile):
        source, at = divmod(number, per_part)
        key_scr[number * tile : (number + 1) * tile, :] = extended(
            qkv_ref[source, HD : 2 * HD, at * tile : (at + 1) * tile],
            tile,
            block_count,
            number * per_tile,
            0,
        )

    def query_tile(number, carried):
        source = number // per_part
        at = pl.multiple_of((number % per_part) * tile, tile)
        bias = block_bias(starts_ref, number * per_tile, tile, block_count)
        query = padded([qkv_ref[source, 0:HD, pl.ds(at, tile)], bias], tile)

        def key_tile(key_number, state):
            largest, total, result = state
            keys = key_scr[pl.ds(pl.multiple_of(key_number * tile, tile), tile), :]
            scores = dot(keys, query)
            key_at = pl.multiple_of((key_number % per_part) * tile, tile)
            values = qkv_ref[key_number // per_part, 2 * HD : 3 * HD, pl.ds(key_at, tile)]
            newest = jnp.maximum(largest, jnp.max(scores, axis=0, keepdims=True))
            factor = jnp.exp(largest - newest)
            weights = jnp.exp(scores - newest)
            total = total * factor + jnp.sum(weights, axis=0, keepdims=True)
            result = result * factor + dot(values, weights.astype(bf16))
            return newest, total, result

        largest, total, result = lax.fori_loop(
            starts_ref[number * per_tile] // per_tile,
            number + 1,
            key_tile,
            (
                jnp.full((1, tile), -jnp.inf, f32),
                jnp.zeros((1, tile), f32),
                jnp.zeros((HD, tile), f32),
            ),
        )
        out_ref[source, :, pl.ds(at, tile)] = result / total
        lse_ref[source, :, pl.ds(at, tile)] = largest + jnp.log(total)
        return carried

    lax.fori_loop(0, tokens // tile, query_tile, 0)


def backward_kernel(
    starts_ref,
    place_ref,
    scale_ref,
    qkv_ref,
    go_ref,
    out_ref,
    lse_ref,
    *refs,
    tokens,
    part,
    tile,
    rows,
):
    pieces = refs[: -6]
    dim_ref, grad_ref, key_scr, value_scr, key_grad, value_grad = refs[-6:]
    block_count = tokens // BLK
    per_part = part // tile
    per_tile = tile // BLK
    for number in range(tokens // tile):
        source, at = divmod(number, per_part)
        columns = slice(at * tile, (at + 1) * tile)
        band = slice(number * tile, (number + 1) * tile)
        key_scr[band, :] = extended(
            qkv_ref[source, HD : 2 * HD, columns], tile, block_count, number * per_tile, 3
        )
        value_scr[band, :] = extended(qkv_ref[source, 2 * HD : 3 * HD, columns], tile, 0, 0, 3)
    key_grad[...] = jnp.zeros_like(key_grad)
    value_grad[...] = jnp.zeros_like(value_grad)

    def query_tile(number, dim_total):
        source = number // per_part
        at = pl.multiple_of((number % per_part) * tile, tile)
        query_t = qkv_ref[source, 0:HD, pl.ds(at, tile)]
        go_t = go_ref[source, :, pl.ds(at, tile)]
        delta = jnp.sum(
            go_t.astype(f32) * out_ref[source, :, pl.ds(at, tile)], axis=0, keepdims=True
        )
        lse = lse_ref[source, :, pl.ds(at, tile)]
        bias = block_bias(starts_ref, number * per_tile, tile, block_count)
        query_ext = padded([query_t, bias] + three_terms(-lse), tile)
        go_ext = padded([go_t] + three_terms(-delta), tile)
        query = padded([query_t], tile).T
        go = padded([go_t], tile).T

        def key_tile(key_number, total):
            band = pl.ds(pl.multiple_of(key_number * tile, tile), tile)
            key_at = pl.multiple_of((key_number % per_part) * tile, tile)
            keys_t = qkv_ref[key_number // per_part, HD : 2 * HD, pl.ds(key_at, tile)]
            weights = jnp.exp(dot(key_scr[band, :], query_ext))
            slopes = (weights * dot(value_scr[band, :], go_ext)).astype(bf16)
            value_grad[band, :] += dot(weights.astype(bf16), go)
            key_grad[band, :] += dot(slopes, query)
            return total + dot(keys_t, slopes)

        grad = lax.fori_loop(
            starts_ref[number * per_tile] // per_tile,
            number + 1,
            key_tile,
            jnp.zeros((HD, tile), f32),
        )
        grad_ref[source, 0:HD, pl.ds(at, tile)] = (grad * scale_ref[...]).astype(bf16)
        return dim_total + jnp.sum(grad * query_t.astype(f32), axis=1, keepdims=True)

    dim_ref[...] = lax.fori_loop(0, tokens // tile, query_tile, jnp.zeros((HD, 1), f32))
    for number in range(tokens // tile):
        source, at = divmod(number, per_part)
        columns = slice(at * tile, (at + 1) * tile)
        band = slice(number * tile, (number + 1) * tile)
        grad_ref[source, HD : 2 * HD, columns] = key_grad[band, :].T[:HD].astype(bf16)
        grad_ref[source, 2 * HD : 3 * HD, columns] = value_grad[band, :].T[:HD].astype(bf16)
    half = pieces[0].shape[1]
    for number, piece in enumerate(pieces):
        flip, at = number % rows, number // rows
        piece[...] = grad_ref[
            jnp.bitwise_xor(place_ref[0], flip), :, at * half : (at + 1) * half
        ]


in_vmem = pl.BlockSpec(memory_space=pltpu.VMEM)
in_smem = pl.BlockSpec(memory_space=pltpu.SMEM)


def attend(starts, place, pieces, rows, part, tile):
    tokens = rows * part
    return pl.pallas_call(
        functools.partial(forward_kernel, tokens=tokens, part=part, tile=tile, rows=rows),
        out_shape=(
            jax.ShapeDtypeStruct((rows, HD, part), f32),
            jax.ShapeDtypeStruct((rows, 1, part), f32),
            jax.ShapeDtypeStruct((rows, 3 * HD, part), bf16),
        ),
        in_specs=[in_smem] * 2 + [in_vmem] * len(pieces),
        out_specs=(in_vmem,) * 3,
        scratch_shapes=[pltpu.VMEM((tokens, LANES), bf16)],
        compiler_params=pltpu.CompilerParams(vmem_limit_bytes=60 << 20),
        cost_estimate=pl.CostEstimate(
            flops=3 * LANES * tokens * tokens,
            bytes_accessed=12 << 20,
            transcendentals=tokens * tokens // 3,
        ),
    )(starts, place, *pieces)


def attend_back(starts, place, scale, qkv, go, out, lse, tile, half):
    rows, _, part = qkv.shape
    tokens = rows * part
    count = rows * (part // half)
    results = pl.pallas_call(
        functools.partial(backward_kernel, tokens=tokens, part=part, tile=tile, rows=rows),
        out_shape=(jax.ShapeDtypeStruct((3 * HD, half), bf16),) * count
        + (jax.ShapeDtypeStruct((HD, 1), f32),),
        in_specs=[in_smem] * 2 + [in_vmem] * 5,
        out_specs=(in_vmem,) * (count + 1),
        scratch_shapes=[pltpu.VMEM((rows, 3 * HD, part), bf16)]
        + [pltpu.VMEM((tokens, LANES), bf16)] * 2
        + [pltpu.VMEM((tokens, LANES), f32)] * 2,
        compiler_params=pltpu.CompilerParams(vmem_limit_bytes=60 << 20),
        cost_estimate=pl.CostEstimate(
            flops=8 * LANES * tokens * tokens,
            bytes_accessed=16 << 20,
            transcendentals=tokens * tokens // 3,
        ),
    )(starts, place, scale.reshape(HD, 1), qkv, go, out, lse)
    return results[:-1], results[-1]


def assemble_kernel(place_ref, group_ref, *refs, cols, splits):
    blocks, out_ref = refs[:-1], refs[-1]
    part = out_ref.shape[1] // len(blocks)
    width = out_ref.shape[2] // cols
    for number, block in enumerate(blocks):
        row = jnp.bitwise_xor(place_ref[0], number // splits)
        piece = jnp.bitwise_xor(group_ref[0], number % splits)
        band = pl.ds(pl.multiple_of((row * splits + piece) * part, 16), part)
        for col in range(cols):
            value = block[col, 0:part, :]
            for matrix in range(3):
                out_ref[matrix, band, col * width : (col + 1) * width] = value[
                    :, matrix * width : (matrix + 1) * width
                ]


def feed_kernel(
    here_ref,
    att_ref,
    normed_ref,
    inverse_ref,
    gains_ref,
    w_ref,
    *refs,
    rows,
    cols,
    heads,
    twins,
):
    go_pieces, change_pieces = refs[:cols], refs[cols : 2 * cols]
    (
        back_ref,
        gain_ref,
        leave_ref,
        go_ref,
        attended,
        normed_two,
        act_ref,
        grad_up_ref,
        branch_grad,
        branch,
        middle,
        grad_two,
        flipped,
        flipped_go,
        grad_att,
        change_ref,
    ) = refs[2 * cols :]
    width, sub = go_pieces[0].shape

    def ring(shift):
        return pl.ds(pl.multiple_of(lax.rem(here_ref[0] + shift, cols) * width, 16), width)

    for number, piece in enumerate(go_pieces):
        go_ref[ring(cols - number), :] = piece[...]
    step = 256
    for col in range(cols):
        for head in range(heads):
            at = (col * heads + head) * HD
            attended[at : at + HD, :] = att_ref[head * twins * cols + col]
    inverse = inverse_ref[...]

    def part(number):
        return pl.ds(pl.multiple_of(number * step, step), step)

    def first(number, total):
        at = part(number)
        here = dot(w_ref[0, at, :], attended[...])
        branch[at, :] = here
        mid = normed_ref[at, :].astype(f32) / (inverse * gains_ref[at, 0:1]) + here
        middle[at, :] = mid
        flipped_go[:, at] = go_ref[at, :].T
        return total + jnp.sum(mid * mid, axis=0, keepdims=True)

    steps = D // step
    total = lax.fori_loop(0, steps, first, jnp.zeros((1, sub), f32))
    inverse_two = lax.rsqrt(total / D + epsilon)

    def second(number, carried):
        at = part(number)
        value = (middle[at, :] * inverse_two * gains_ref[at, 1:2]).astype(bf16)
        normed_two[at, :] = value
        flipped[:, at] = value.T
        return carried

    lax.fori_loop(0, steps, second, 0)

    def third(number, carried):
        at = part(number)
        up_proj = dot(flipped[...], w_ref[1, :, at])
        sigmoid_up = jax.nn.sigmoid(up_proj)
        act_ref[:, at] = (up_proj * sigmoid_up).astype(bf16)
        grad_act = dot(flipped_go[...], w_ref[2, :, at])
        grad_up_ref[:, at] = (
            grad_act * sigmoid_up * (1.0 + up_proj * (1.0 - sigmoid_up))
        ).astype(bf16)
        return carried

    lax.fori_loop(0, steps, third, 0)

    def fourth(number, along):
        at = part(number)
        change_ref[at, :] = (branch[at, :] + dot_last(w_ref[2, at, :], act_ref[...])).astype(bf16)
        grad = dot_last(w_ref[1, at, :], grad_up_ref[...])
        grad_two[at, :] = grad
        return along + jnp.sum(gains_ref[at, 1:2] * grad * middle[at, :], axis=0, keepdims=True)

    along = lax.fori_loop(0, steps, fourth, jnp.zeros((1, sub), f32))
    shrink = inverse_two * inverse_two * inverse_two * along / D

    def fifth(number, carried):
        at = part(number)
        grad = grad_two[at, :]
        mid = middle[at, :]
        back = inverse_two * gains_ref[at, 1:2] * grad - mid * shrink
        back_ref[at, :] = back / (inverse * gains_ref[at, 0:1])
        gain_ref[at, :] = jnp.sum(grad * mid * inverse_two, axis=1, keepdims=True)
        value = (go_ref[at, :].astype(f32) + back).astype(bf16)
        branch_grad[at, :] = value
        flipped[:, at] = value.T
        return carried

    lax.fori_loop(0, steps, fifth, 0)

    def sixth(number, carried):
        at = part(number)
        grad_att[at, :] = dot(flipped[...], w_ref[0, :, at]).T.astype(bf16)
        return carried

    lax.fori_loop(0, steps, sixth, 0)
    for number, piece in enumerate(change_pieces):
        piece[...] = change_ref[ring(number), :]
    for row in range(rows):
        for col in range(cols):
            at = (col * heads + row // twins) * HD
            leave_ref[row * cols + col] = grad_att[at : at + HD, :]


def dot_last(left, right):
    return lax.dot_general(left, right, (((1,), (1,)), ((), ())), preferred_element_type=f32)


def weights_kernel(
    place_ref, branch_grad, attended, normed_two, grad_up, go, act, *outs, cols, order
):
    share, wide = outs[0].shape[-2:]
    width = wide // 3
    for slot, (out, at) in enumerate(order):
        row = jnp.bitwise_xor(place_ref[0], slot)
        band = pl.ds(pl.multiple_of(row * share, 16), share)
        for number, value in enumerate(
            (
                dot_last(branch_grad[band, :], attended[...]),
                dot(normed_two[band, :], grad_up[...]),
                dot(go[band, :], act[...]),
            )
        ):
            value = value.astype(bf16)
            for col in range(cols):
                outs[out][col, at, :, number * width : (number + 1) * width] = value[
                    :, col * width : (col + 1) * width
                ]


def assemble(place, group, blocks, splits):
    cols = blocks[0].shape[0]
    return pl.pallas_call(
        functools.partial(assemble_kernel, cols=cols, splits=splits),
        out_shape=jax.ShapeDtypeStruct((3, D, D), bf16),
        in_specs=[in_smem] * 2 + [in_vmem] * len(blocks),
        out_specs=in_vmem,
        compiler_params=pltpu.CompilerParams(vmem_limit_bytes=60 << 20),
        cost_estimate=pl.CostEstimate(flops=0, bytes_accessed=20 << 20, transcendentals=0),
    )(place, group, *blocks)


def feed_forward(here, attended, pieces, normed, inverse, gains, weights, rows, cols, heads, twins):
    width, sub = pieces[0].shape
    flat = jax.ShapeDtypeStruct((D, sub), bf16)
    turned = jax.ShapeDtypeStruct((sub, D), bf16)
    results = pl.pallas_call(
        functools.partial(feed_kernel, rows=rows, cols=cols, heads=heads, twins=twins),
        out_shape=(jax.ShapeDtypeStruct((width, sub), bf16),) * cols
        + (
            jax.ShapeDtypeStruct((D, sub), f32),
            jax.ShapeDtypeStruct((D, 1), f32),
            jax.ShapeDtypeStruct((rows * cols, HD, sub), bf16),
            flat,
            flat,
            flat,
            turned,
            turned,
            flat,
        ),
        in_specs=[in_smem] + [in_vmem] * (5 + cols),
        out_specs=(in_vmem,) * (cols + 9),
        scratch_shapes=[pltpu.VMEM((D, sub), f32)] * 3
        + [pltpu.VMEM((sub, D), bf16)] * 2
        + [pltpu.VMEM((D, sub), bf16)] * 2,
        compiler_params=pltpu.CompilerParams(vmem_limit_bytes=60 << 20),
        cost_estimate=pl.CostEstimate(
            flops=12 * D * D * sub, bytes_accessed=20 << 20, transcendentals=D * sub
        ),
    )(here, attended, normed, inverse, gains, weights, *pieces)
    return results[:cols], results[cols:]


def weight_grads(place, branch_grad, attended, normed_two, grad_up, go, act, shapes, order):
    cols = shapes[0][0]
    sub = go.shape[1]
    return pl.pallas_call(
        functools.partial(weights_kernel, cols=cols, order=order),
        out_shape=tuple(jax.ShapeDtypeStruct(shape, bf16) for shape in shapes),
        in_specs=[in_smem] + [in_vmem] * 6,
        out_specs=(in_vmem,) * len(shapes),
        compiler_params=pltpu.CompilerParams(vmem_limit_bytes=60 << 20),
        cost_estimate=pl.CostEstimate(
            flops=6 * D * D * sub, bytes_accessed=16 << 20, transcendentals=0
        ),
    )(place, branch_grad, attended, normed_two, grad_up, go, act)


def copies_kernel(place_ref, *refs):
    blocks, (whole, turned) = refs[:-2], refs[-2:]
    share = blocks[0].shape[0]
    for flip, block in enumerate(blocks):
        row = jnp.bitwise_xor(place_ref[0], flip)
        whole[pl.ds(pl.multiple_of(row * share, 16), share), :] = block[...]
    for number in range(D // LANES):
        at = slice(number * LANES, (number + 1) * LANES)
        turned[:, at] = whole[at, :].T


def projection_copies(place, blocks):
    share, wide = blocks[0].shape
    return pl.pallas_call(
        copies_kernel,
        out_shape=(
            jax.ShapeDtypeStruct((D, wide), bf16),
            jax.ShapeDtypeStruct((wide, D), bf16),
        ),
        in_specs=[in_smem] + [in_vmem] * len(blocks),
        out_specs=(in_vmem,) * 2,
        compiler_params=pltpu.CompilerParams(vmem_limit_bytes=60 << 20),
        cost_estimate=pl.CostEstimate(flops=0, bytes_accessed=8 << 20, transcendentals=0),
    )(place, *blocks)


def project_kernel(here_ref, place_ref, turned_ref, factor_ref, *refs, rows, cols, heads):
    own, right, left = refs[0], refs[1:cols], refs[cols : 2 * cols - 1]
    outs, normed, result = refs[2 * cols - 1 : -2], refs[-2], refs[-1]
    width = own.shape[0]
    here = here_ref[0]

    def block(number):
        return pl.ds(pl.multiple_of(number * width, 16), width)

    normed[block(here), :] = own[...]
    for step in range(1, cols):

        @pl.when(here >= step)
        def _():
            normed[block(here - step), :] = right[step - 1][...]

        @pl.when(here + step < cols)
        def _():
            normed[block(here + step), :] = left[step - 1][...]

    for head in range(heads):
        at = slice(head * 3 * HD, (head + 1) * 3 * HD)
        value = dot(turned_ref[at, :], normed[...]) * factor_ref[at, :]
        result[head] = value.astype(bf16)
    for flip, out in enumerate(outs):
        out[...] = result[jnp.bitwise_xor(place_ref[0], flip) // (rows // heads)]


def project(here, place, turned, factors, pieces, rows, cols, heads):
    width, half = pieces[0].shape
    results = pl.pallas_call(
        functools.partial(project_kernel, rows=rows, cols=cols, heads=heads),
        out_shape=(jax.ShapeDtypeStruct((3 * HD, half), bf16),) * rows
        + (jax.ShapeDtypeStruct((D, half), bf16),),
        in_specs=[in_smem] * 2 + [in_vmem] * (2 + len(pieces)),
        out_specs=(in_vmem,) * (rows + 1),
        scratch_shapes=[pltpu.VMEM((heads, 3 * HD, half), bf16)],
        compiler_params=pltpu.CompilerParams(vmem_limit_bytes=60 << 20),
        cost_estimate=pl.CostEstimate(
            flops=2 * D * 3 * width * half, bytes_accessed=10 << 20, transcendentals=0
        ),
    )(here, place, turned, factors, *pieces)
    return results[:-1], results[-1]


def back_kernel(
    here_ref, place_ref, whole_ref, normed_ref, back_ref, *refs, rows, cols, heads, first
):
    pieces, (own, right, left) = refs[:rows], (refs[rows], refs[rows + 1 : rows + cols], refs[rows + cols : -2])
    grads, payload = refs[-2], refs[-1]
    half = normed_ref.shape[1]
    width = D // cols
    sub = back_ref.shape[1]
    here = here_ref[0]
    for flip, piece in enumerate(pieces):
        head = jnp.bitwise_xor(place_ref[0], flip) // (rows // heads)
        grads[pl.ds(pl.multiple_of(head * 3 * HD, 16), 3 * HD), :] = piece[...]
    along = jnp.zeros((1, half), f32)
    for col in range(cols):
        at = slice(col * width, (col + 1) * width)
        value = dot(whole_ref[at, :], grads[...])
        along += jnp.sum(value * normed_ref[at, :].astype(f32), axis=0, keepdims=True)
        payload[col, 0:width, :] = value.astype(bf16)
        for number in range(half // sub):

            @pl.when(here == first + number)
            def _():
                columns = slice(number * sub, (number + 1) * sub)
                payload[col, 0:width, columns] = (value[:, columns] + back_ref[at, :]).astype(bf16)

    tail = jnp.concatenate([along, jnp.zeros((15, half), f32)], axis=0).astype(bf16)
    for col in range(cols):
        payload[col, width : width + 16, :] = tail
    own[...] = payload[here]
    for step in range(1, cols):

        @pl.when(here + step < cols)
        def _():
            right[step - 1][...] = payload[here + step]

        @pl.when(here >= step)
        def _():
            left[step - 1][...] = payload[here - step]


def project_back(here, place, whole, normed, back, pieces, rows, cols, heads, first):
    half = normed.shape[1]
    width = D // cols
    block = jax.ShapeDtypeStruct((width + 16, half), bf16)
    results = pl.pallas_call(
        functools.partial(
            back_kernel, rows=rows, cols=cols, heads=heads, first=first
        ),
        out_shape=(block,) * (2 * cols - 1) + (jax.ShapeDtypeStruct((3 * width, half), bf16),),
        in_specs=[in_smem] * 2 + [in_vmem] * (3 + rows),
        out_specs=(in_vmem,) * (2 * cols),
        scratch_shapes=[pltpu.VMEM((cols, width + 16, half), bf16)],
        compiler_params=pltpu.CompilerParams(vmem_limit_bytes=60 << 20),
        cost_estimate=pl.CostEstimate(
            flops=2 * D * 3 * width * half, bytes_accessed=12 << 20, transcendentals=0
        ),
    )(here, place, whole, normed, back, *pieces)
    return results[0], results[1:cols], results[cols:-1], results[-1]


def projection_grads_kernel(place_ref, whole_ref, *refs, order):
    outs, gain_ref = refs[-1 - (max(out for out, _ in order) + 1) : -1], refs[-1]
    pairs = refs[: len(refs) - 1 - len(outs)]
    share = outs[0].shape[1]
    for slot, (out, at) in enumerate(order):
        row = jnp.bitwise_xor(place_ref[0], slot)
        band = pl.ds(pl.multiple_of(row * share, 16), share)
        value = sum(
            dot_last(pairs[2 * number][band, :], pairs[2 * number + 1][...])
            for number in range(len(pairs) // 2)
        )
        gain_ref[band, :] = jnp.sum(value * whole_ref[band, :].astype(f32), axis=1, keepdims=True)
        outs[out][at] = value.astype(bf16)


def projection_grads(place, whole, pairs, shapes, order):
    flops = 2 * D * whole.shape[1] * sum(pair.shape[1] for pair in pairs[::2])
    return pl.pallas_call(
        functools.partial(projection_grads_kernel, order=order),
        out_shape=tuple(jax.ShapeDtypeStruct(shape, bf16) for shape in shapes)
        + (jax.ShapeDtypeStruct((D, 1), f32),),
        in_specs=[in_smem] + [in_vmem] * (1 + len(pairs)),
        out_specs=(in_vmem,) * (len(shapes) + 1),
        compiler_params=pltpu.CompilerParams(vmem_limit_bytes=60 << 20),
        cost_estimate=pl.CostEstimate(flops=flops, bytes_accessed=12 << 20, transcendentals=0),
    )(place, whole, *pairs)


def after(values, *others):
    return lax.optimization_barrier((values,) + others)[0]


def partner(values, flip, size, axis="row"):
    return lax.ppermute(values, axis, [(at, at ^ flip) for at in range(size)])


def swapped(pieces, rows):
    return [pieces[0]] + [partner(pieces[flip], flip, rows) for flip in range(1, rows)]


def spread_rows(values, rows):
    if rows != 4:
        return swapped([values] * rows, rows)
    far = partner(values, 2, rows)
    return [values, partner(values, 1, rows), far, partner(far, 1, rows)]


class LineScatter:
    def __init__(self, own, right, left, cols):
        self.own, self.right, self.left, self.cols = own, right, left, cols
        self.moving = [right[-1], left[-1]]
        self.left_steps = cols - 1

    def step(self, *ties):
        step, cols = self.left_steps, self.cols
        to_right, to_left = (after(value, *ties) if ties else value for value in self.moving)
        from_left = lax.ppermute(to_right, "col", [(at, at + 1) for at in range(cols - step)])
        from_right = lax.ppermute(to_left, "col", [(at, at - 1) for at in range(step, cols)])
        if step > 1:
            self.moving = [
                add(self.right[step - 2], from_left).astype(bf16),
                add(self.left[step - 2], from_right).astype(bf16),
            ]
        else:
            self.total = self.own.astype(f32) + add(from_left, from_right)
        self.left_steps -= 1
        return from_left


def add(left, right):
    return left.astype(f32) + right.astype(f32)


def total(values, axes):
    for axis, size in axes:
        flip = 1
        while flip < size:
            values = values + partner(values, flip, size, axis)
            flip *= 2
    return values


def sum_groups(values, groups):
    if groups == 2:
        return add(values, partner(values, 1, 2, "dp"))
    return lax.psum(values, "dp").astype(f32)


def line_gather(piece, cols):
    right, left = [], []
    to_right = to_left = piece
    for step in range(1, cols):
        to_right = lax.ppermute(to_right, "col", [(at, at + 1) for at in range(step - 1, cols - 1)])
        to_left = lax.ppermute(to_left, "col", [(at, at - 1) for at in range(1, cols - step + 1)])
        right.append(to_right)
        left.append(to_left)
    return [piece] + right + left


def ring_swap(pieces, cols):
    return [pieces[0]] + [
        lax.ppermute(pieces[shift], "col", [(at, (at + shift) % cols) for at in range(cols)])
        for shift in range(1, cols)
    ]


def on_device(
    groups, rows, cols, residual_in, seq_ids, norm1_gain, w_qkv, per_dim, w_out, norm2_gain, w_up, w_down, out_grad
):
    count, width = residual_in.shape
    heads = width // HD
    twins = rows // heads
    sub = count // cols
    half = count // 2
    share = w_qkv.shape[0]
    tile = 768 if count % 768 == 0 else BLK
    here = lax.axis_index("col")
    place = lax.axis_index("row")
    here_of, place_of = here[None].astype(jnp.int32), place[None].astype(jnp.int32)

    block_seq = seq_ids[::BLK]
    starts = jnp.sum((block_seq[None, :] < block_seq[:, None]).astype(jnp.int32), axis=1)

    residual = residual_in.T
    squares = jnp.sum(residual * residual, axis=0)
    squares = squares + partner(squares, 1, cols, "col")
    inverse_one = lax.rsqrt((squares + partner(squares, 2, cols, "col")) / D + epsilon)[None, :]
    normed = (residual * inverse_one * norm1_gain[:, None]).astype(bf16)

    stacked = jnp.concatenate(
        [w_out.T, w_up, w_down.T], axis=1
    ).astype(bf16)
    gains = [jnp.concatenate(three_terms(gain))[None] for gain in (norm1_gain, norm2_gain)]
    splits = 2 if groups == 2 and rows == 4 else 1
    part = share // splits
    group_of = jnp.zeros((1,), jnp.int32)
    if splits == 2:
        group = lax.axis_index("dp")
        group_of = group[None].astype(jnp.int32)
        stacked = lax.dynamic_slice_in_dim(stacked, group * part, part, 0)
    stacked = jnp.concatenate([stacked] + gains + [jnp.zeros((14, 3 * width), bf16)], axis=0)
    gathered = lax.all_gather(stacked, "col", axis=0)
    gains = gathered[:, part : part + 2].astype(f32).reshape(cols, 2, 3, width).sum(axis=2)
    gains = gains.transpose(0, 2, 1).reshape(D, 2)

    qkv_local = w_qkv.astype(bf16).reshape(share, 3, heads, HD).transpose(0, 2, 1, 3)
    qkv_local = qkv_local.reshape(share, heads * 3 * HD)
    whole, turned = projection_copies(place_of, spread_rows(qkv_local, rows))
    scale = jax.nn.softplus(per_dim) * scale_base / math.sqrt(HD)
    factors = jnp.tile(jnp.concatenate([scale, jnp.ones((2 * HD,), f32)]), heads)[:, None]
    pieces, normed_parts = [], []
    for at in range(2):
        blocks = line_gather(normed[:, at * half : (at + 1) * half], cols)
        outs, normed_part = project(here_of, place_of, turned, factors, blocks, rows, cols, heads)
        pieces += swapped(outs, rows)
        normed_parts.append(normed_part)

    if splits == 2:
        far = partner(gathered, 2, rows)
        near = [gathered, partner(gathered, 1, 2, "dp"), far, partner(far, 1, 2, "dp")]

    result, lse, qkv_heads = attend(starts, place_of, pieces, rows, count, tile)
    if splits == 2:
        other = [partner(after(value, lse), 1, rows) for value in near]
        blocks = near[:2] + other[:2] + near[2:] + other[2:]
    else:
        blocks = spread_rows(gathered, rows)
    weights = assemble(place_of, group_of, blocks, splits)
    leaving = result.astype(bf16).reshape(rows, HD, cols, sub).transpose(0, 2, 1, 3)
    arrived = lax.all_to_all(leaving.reshape(rows * cols, HD, sub), ("row", "col"), 0, 0, tiled=True)

    out_grad_t = out_grad.T.astype(bf16)

    def quarter(values, shift):
        at = lax.rem(here + shift, cols) * sub
        return lax.dynamic_slice_in_dim(values, at, sub, 1)

    grad_pieces = ring_swap([quarter(out_grad_t, shift) for shift in range(cols)], cols)
    own_inverse = quarter(inverse_one, 0)
    own_at = lax.rem(here, cols // 2) * sub
    own_normed = jnp.where(
        here < cols // 2,
        lax.dynamic_slice_in_dim(normed_parts[0], own_at, sub, 1),
        lax.dynamic_slice_in_dim(normed_parts[1], own_at, sub, 1),
    )
    change, (
        back_two,
        gain_two_part,
        leaving,
        grad_mlp,
        attended,
        normed_two,
        activated,
        grad_up,
        grad_branch,
    ) = feed_forward(
        here_of, arrived, grad_pieces, own_normed, own_inverse, gains, weights, rows, cols, heads, twins
    )

    arrived = lax.all_to_all(leaving, ("row", "col"), 0, 0, tiled=True)
    go = arrived.reshape(rows, cols, HD, sub).transpose(0, 2, 1, 3).reshape(rows, HD, count)

    change = ring_swap([after(piece, go) for piece in change], cols)

    wide = (share, 3 * width)
    operands = (grad_branch, attended, normed_two, grad_up, grad_mlp, activated)
    if rows == 4:
        kept, sent = weight_grads(
            place_of,
            *operands,
            ((cols, 2) + wide,) * 2,
            ((0, 0), (1, 0), (0, 1), (1, 1)),
        )
        arrived = after(partner(sent, 1, rows), go)
        mine = add(kept, arrived).astype(bf16).reshape(cols, 2 * share, 3 * width)
        go = after(go, mine)
    else:
        (mine,) = weight_grads(
            jnp.zeros((1,), jnp.int32),
            *operands,
            ((cols, rows) + wide,),
            tuple((0, row) for row in range(rows)),
        )
        mine = lax.psum_scatter(mine, "row", scatter_dimension=1, tiled=False)

    pieces, dim_part = attend_back(
        starts, place_of, scale, qkv_heads, go, result, lse, tile, half
    )
    mine = lax.psum_scatter(mine, "col", scatter_dimension=0, tiled=False)
    if rows == 4:
        mine = mine.reshape((2,) + wide)
        mine = add(mine[0], partner(mine[1], 2, rows)).astype(bf16)
    shard = sum_groups(mine.reshape(wide), groups)

    arrived = []
    for at in range(2):
        leaving = [after(piece, *change) for piece in pieces[at * rows : (at + 1) * rows]]
        arrived.append(swapped(leaving, rows))
    blocks, pairs = [], []
    for at in range(2):
        own, right, left, grads = project_back(
            here_of,
            place_of,
            whole,
            normed_parts[at],
            back_two,
            arrived[at],
            rows,
            cols,
            heads,
            at * (cols // 2),
        )
        blocks.append(LineScatter(own, right, left, cols))
        pairs += [normed_parts[at], grads]

    first, second = blocks
    mark = first.step()
    second.step()
    pairs[1] = after(pairs[1], mark)
    own_head = (place % twins == 0).astype(f32)
    if rows == 4:
        kept, sent, gain_one_part = projection_grads(
            place_of, whole, pairs, ((2,) + wide,) * 2, ((0, 0), (1, 0), (0, 1), (1, 1))
        )
        arrived = partner(sent, 1, rows)
    else:
        mine, gain_one_part = projection_grads(
            jnp.zeros((1,), jnp.int32),
            whole,
            pairs,
            ((rows,) + wide,),
            tuple((0, row) for row in range(rows)),
        )
        arrived = lax.psum_scatter(mine, "row", scatter_dimension=0, tiled=False)
    small = jnp.concatenate([gain_one_part, gain_two_part, dim_part * own_head])[:, 0]
    first.step()
    second.step(arrived)
    if rows == 4:
        far = partner(add(kept[1], arrived[1]).astype(bf16), 2, rows)
        mine = (add(kept[0], arrived[0]) + far.astype(f32)).astype(bf16)
    else:
        far = mine = arrived
    small = total(small, (("row", rows), ("dp", groups)))
    small = small + partner(small, 1, cols, "col")
    first.step(far)
    second.step(far)
    qkv_grad = sum_groups(mine, groups)
    qkv_grad = qkv_grad.reshape(share, heads, 3, HD).transpose(0, 2, 1, 3).reshape(share, 3, width)
    small = small + partner(small, 2, cols, "col")
    gain_one_grad = lax.dynamic_slice_in_dim(small[:D], here * width, width) / norm1_gain
    gain_two_grad = lax.dynamic_slice_in_dim(small[D : 2 * D], here * width, width)
    scale_grad = small[2 * D :] / scale * (scale_base / math.sqrt(HD)) * jax.nn.sigmoid(per_dim)

    output = jnp.zeros_like(residual_in)
    for shift, piece in enumerate(change):
        at = lax.rem(here + cols - shift, cols) * sub
        piece = lax.dynamic_slice_in_dim(residual_in, at, sub, 0) + after(piece, mark).astype(f32).T
        output = lax.dynamic_update_slice_in_dim(output, piece, at, 0)

    summed = jnp.concatenate([first.total, second.total], axis=1)
    grad_one, along_one = summed[:width], summed[width : width + 1]
    back_one = inverse_one * norm1_gain[:, None] * grad_one - residual * inverse_one**2 * (
        along_one / D
    )
    input_grad = out_grad + back_one.T
    return (
        output,
        input_grad,
        gain_one_grad,
        qkv_grad,
        scale_grad,
        shard[:, :width].T,
        gain_two_grad,
        shard[:, width : 2 * width],
        shard[:, 2 * width :].T,
    )


def solution(mesh):
    in_specs = (
        P(("dp", "row"), "col"),
        P("dp"),
        P("col"),
        P("row", None, "col"),
        P(),
        P("col", "row"),
        P("col"),
        P("row", "col"),
        P("col", "row"),
        P(("dp", "row"), "col"),
    )
    out_specs = (
        P(("dp", "row"), "col"),
        P(("dp", "row"), "col"),
        P("col"),
        P("row", None, "col"),
        P(),
        P("col", "row"),
        P("col"),
        P("row", "col"),
        P("col", "row"),
    )
    return jax.shard_map(
        functools.partial(on_device, mesh.shape["dp"], mesh.shape["row"], mesh.shape["col"]),
        mesh=mesh,
        in_specs=in_specs,
        out_specs=out_specs,
        check_vma=False,
    )
```

time: 815 us -> 559 us (0.69)
  waiting for transfers between devices: 375 us -> 143 us
  Pallas kernels: 75 us -> 176 us
  starting transfers between devices: 30.9 us -> 118 us
  local copies, waits for them, and re-layouts: 112 us -> 26.1 us
  blocking collectives: 119 us -> 34.2 us
  matrix products: 58.7 us -> 0 us
  other arithmetic: 19.5 us -> 43.6 us
    all_to_all x6 -> x0, waiting for transfers between devices: 165 us -> none  [the longest x2 66.2 us: collect(): lax.all_to_all(values.reshape(cols, width, sub), 'col', 0, 0, tiled=True)]
    ppermute x0 -> x65, waiting for transfers between devices: none -> 143 us  [the longest x35 72.2 us: partner(): return lax.ppermute(values, axis, [(at, at ^ flip) for at in range(size)])]
    ppermute x0 -> x65, starting transfers between devices: none -> 114 us  [the longest x35 48.5 us: partner(): return lax.ppermute(values, axis, [(at, at ^ flip) for at in range(size)])]
    pallas_call x0 -> x9, Pallas kernels: none -> 93 us  [the longest x1 24.5 us: feed_forward(): pl.pallas_call(functools.partial(feed_kernel, rows=rows, cols=cols, heads...]
    all_gather x3 -> x1, waiting for transfers between devices: 89.1 us -> 0.01 us  [on_device(): gathered = lax.all_gather(stacked, 'col', axis=0)]
    psum x3 -> x0, blocking collectives: 86.2 us -> none  [the longest x1 61.5 us: on_device(): small = lax.psum(small, ('dp', 'row', 'col'))]
    reduce_scatter x2 -> x1, waiting for transfers between devices: 73.7 us -> 0.02 us  [on_device(): mine = lax.psum_scatter(mine, 'col', scatter_dimension=0, tiled=False)]
    dot_general x12 -> x0, matrix products: 58.7 us -> none  [product(): return jnp.einsum(form, left, right, preferred_element_type=f32)]
  transfers between devices with their start and end apart: 14 -> 68, of which waited for: 9 -> 26; matrix products, arithmetic and copies ran while one was open for 18% -> 9% of each run, Pallas kernels for 4% -> 25%
where the time goes in v2:
time: 559 us; the launch traced here: 556 us
  Pallas kernels  176 us (31%)
  waiting for transfers between devices  143 us (26%)
  starting transfers between devices  118 us (21%)
  other arithmetic  43.6 us (8%)
  blocking collectives  34.2 us (6%)
  local copies, waits for them, and re-layouts  26.1 us (5%)
  between operations  15.4 us (3%)
    ppermute x35, waiting for transfers between devices, partner(): return lax.ppermute(values, axis, [(at, at ^ flip) for at in range(size)])  72.2 us
    pallas_call x1, Pallas kernels, attend_back(): pl.pallas_call(functools.partial(backward_kernel, tokens=tokens, part=par...  49.2 us
    ppermute x35, starting transfers between devices, partner(): return lax.ppermute(values, axis, [(at, at ^ flip) for at in range(size)])  48.5 us
    ppermute x6, waiting for transfers between devices, line_gather(): lax.ppermute(to_left, 'col', [(at, at - 1) for at in range(1, cols - step...  44 us
    all_to_all x1, blocking collectives, on_device(): arrived = lax.all_to_all(leaving, ('row', 'col'), 0, 0, tiled=True)  34.2 us
    pallas_call x1, Pallas kernels, attend(): pl.pallas_call(functools.partial(forward_kernel, tokens=tokens, part=part...  33.5 us
    ppermute x6, starting transfers between devices, step(): lax.ppermute(to_right, 'col', [(at, at + 1) for at in range(cols - step)])  27.8 us
    pallas_call x1, Pallas kernels, feed_forward(): pl.pallas_call(functools.partial(feed_kernel, rows=rows, cols=cols, heads...  24.5 us
  transfers between devices with their start and end apart: 68, of which 26 were waited for; matrix products, arithmetic and copies ran while one was open for 9% of the time, Pallas kernels for 25%

profile of v2, /device:TPU:0, one launch (start us, length us, event | category | flops | bytes accessed | tf_op | source)
XLA Modules:
  0.0 556.1 jit_solution(1470466447073676117)
XLA Ops:
  7.3 1.8 multiply_reduce_fusion
  9.1 3.1 collective-permute-start.3
  13.8 3.0 collective-permute-start.4
  19.7 4.6 collective-permute-start.14
  26.9 1.7 copy.65
  29.0 1.6 collective-permute-start.1
  30.6 6.0 %collective-permute-start.5 = (bf16[320,768]{1,0:T(8,128)(2,1)}, bf16[320,768]{1,0:T(8,128)(2,1)}, u32[]{:S(2)}, u32[]{:S(2)}) collective-permute-start(bf16[320,768]{1,0:T(8,128)(2,1)} %get-tuple-element.233.refs_0_), channel_id=1, source_target_pairs={{0,1},{1,2},{2,3},{4,5},{5,6},{6,7},{8,9},{9,10},{10,11},{12,13},{... | collective-permute-start | bytes 1474568 | tf_op jit(solution)/shard_map/ppermute | solution.py:691
  36.6 8.7 %collective-permute-done.14.refs_1_ = bf16[320,768]{1,0:T(8,128)(2,1)} collective-permute-done((bf16[320,768]{1,0:T(8,128)(2,1)}, bf16[320,768]{1,0:T(8,128)(2,1)}, u32[]{:S(2)}, u32[]{:S(2)}) %collective-permute-start.14) | collective-permute-done | bytes 491552 | tf_op jit(solution)/shard_map/ppermute | solution.py:691
  45.3 14.7 %collective-permute-done.17.refs_4_ = bf16[320,768]{1,0:T(8,128)(2,1)} collective-permute-done((bf16[320,768]{1,0:T(8,128)(2,1)}, bf16[320,768]{1,0:T(8,128)(2,1)}, u32[]{:S(2)}, u32[]{:S(2)}) %collective-permute-start.17) | collective-permute-done | bytes 491552 | tf_op jit(solution)/shard_map/ppermute | solution.py:692
  61.4 9.2 %collective-permute-done.8.refs_4_ = bf16[320,768]{1,0:T(8,128)(2,1)} collective-permute-done((bf16[320,768]{1,0:T(8,128)(2,1)}, bf16[320,768]{1,0:T(8,128)(2,1)}, u32[]{:S(2)}, u32[]{:S(2)}) %collective-permute-start.8) | collective-permute-done | bytes 491552 | tf_op jit(solution)/shard_map/ppermute | solution.py:692
  77.2 9.8 %collective-permute-done.18.refs_5_ = bf16[320,768]{1,0:T(8,128)(2,1)} collective-permute-done((bf16[320,768]{1,0:T(8,128)(2,1)}, bf16[320,768]{1,0:T(8,128)(2,1)}, u32[]{:S(2)}, u32[]{:S(2)}) %collective-permute-start.18) | collective-permute-done | bytes 491552 | tf_op jit(solution)/shard_map/ppermute | solution.py:692
  88.3 9.2 %collective-permute-done.9.refs_5_ = bf16[320,768]{1,0:T(8,128)(2,1)} collective-permute-done((bf16[320,768]{1,0:T(8,128)(2,1)}, bf16[320,768]{1,0:T(8,128)(2,1)}, u32[]{:S(2)}, u32[]{:S(2)}) %collective-permute-start.9) | collective-permute-done | bytes 491552 | tf_op jit(solution)/shard_map/ppermute | solution.py:692
  97.5 1.5 collective-permute-start.26
  102.8 4.1 shard_map.169
  108.0 6.8 %shard_map.171 = (bf16[240,768]{1,0:T(8,128)(2,1)}, bf16[240,768]{1,0:T(8,128)(2,1)}, bf16[240,768]{1,0:T(8,128)(2,1)}, bf16[240,768]{1,0:T(8,128)(2,1)}, bf16[1280,768]{1,0:T(8,128)(2,1)}) custom-call(s32[1]{0:T(128)} %bitcast.here_ref, s32[1]{0:T(128)} %bitcast.1.place_ref, bf16[960,1280]{1,0:T(8,128)(2,1)} %get-tuple-element.96.turned_ref, ...), custom_call_target="tpu_custom_call" | custom-call | flops 1887436800 | bytes 10485760 | tf_op jit(solution)/shard_map/pallas_call | solution.py:524
  114.9 1.6 collective-permute-start.21
  116.7 6.8 %shard_map.170 = (bf16[240,768]{1,0:T(8,128)(2,1)}, bf16[240,768]{1,0:T(8,128)(2,1)}, bf16[240,768]{1,0:T(8,128)(2,1)}, bf16[240,768]{1,0:T(8,128)(2,1)}, bf16[1280,768]{1,0:T(8,128)(2,1)}) custom-call(s32[1]{0:T(128)} %bitcast.here_ref, s32[1]{0:T(128)} %bitcast.1.place_ref, bf16[960,1280]{1,0:T(8,128)(2,1)} %get-tuple-element.96.turned_ref, ...), custom_call_target="tpu_custom_call" | custom-call | flops 1887436800 | bytes 10485760 | tf_op jit(solution)/shard_map/pallas_call | solution.py:524
  125.4 14.7 %collective-permute-done.21.refs_6_ = bf16[240,768]{1,0:T(8,128)(2,1)S(1)} collective-permute-done((bf16[240,768]{1,0:T(8,128)(2,1)}, bf16[240,768]{1,0:T(8,128)(2,1)S(1)}, u32[]{:S(2)}, u32[]{:S(2)}) %collective-permute-start.21) | collective-permute-done | bytes 368672 | tf_op jit(solution)/shard_map/ppermute | solution.py:632
  141.7 5.5 collective-permute-done.22.refs_7_
  149.2 4.5 collective-permute-done.12.refs_2_
  153.7 3.0 collective-permute-done.13.refs_3_
  156.8 33.5 %shard_map.172 = (f32[4,80,1536]{2,1,0:T(8,128)}, f32[4,1,1536]{2,1,0:T(1,128)}, bf16[4,240,1536]{2,1,0:T(8,128)(2,1)}) custom-call(s32[24]{0:T(128)} %convert_reduce_fusion.starts_ref, s32[1]{0:T(128)} %bitcast.1.place_ref, bf16[240,768]{1,0:T(8,128)(2,1)} %get-tuple-element.97.refs_0_, bf16[240,768]{1,0:T(8,128)(2,1)} %copy-done.38, ...), custom_call_target="tpu_custom_call" | custom-call | flops 14495514624 | bytes 12582912 | tf_op jit(solution)/shard_map/pallas_call | solution.py:204
  190.3 1.6 convert_element_type.211
  193.1 4.3 all-to-all-start
  199.4 13.3 %collective-permute-done.27.refs_5_ = bf16[4,176,960]{2,1,0:T(8,128)(2,1)} collective-permute-done((bf16[4,176,960]{2,1,0:T(8,128)(2,1)}, bf16[4,176,960]{2,1,0:T(8,128)(2,1)}, u32[]{:S(2)}, u32[]{:S(2)}) %collective-permute-start.27) | collective-permute-done | bytes 1351712 | tf_op jit(solution)/shard_map/ppermute | solution.py:632
  213.0 1.6 convert_element_type.222
  216.2 3.9 collective-permute-start.32
  220.1 2.7 dynamic-slice_select_fusion.normed_ref
  224.9 10.5 %shard_map.173.w_ref = bf16[3,1280,1280]{2,1,0:T(8,128)(2,1)} custom-call(s32[1]{0:T(128)} %bitcast.1.place_ref, s32[1]{0:T(128)} %bitcast.12.group_ref, bf16[4,176,960]{2,1,0:T(8,128)(2,1)} %bitcast.9.refs_0_, bf16[4,176,960]{2,1,0:T(8,128)(2,1)} %collective-permute-done.23.refs_1_, bf16[4,176,960]{2,1,0:T(8,128)(2,1)} %collective-permute-done.24.refs_2_, ...), custom_call_target="tpu_custom_call" | custom-call | bytes 20971520 | tf_op jit(solution)/shard_map/pallas_call | solution.py:412
  235.4 3.3 collective-permute-done.31.refs_2_
  239.4 24.5 %shard_map.174 = (bf16[320,384]{1,0:T(8,128)(2,1)}, bf16[320,384]{1,0:T(8,128)(2,1)}, bf16[320,384]{1,0:T(8,128)(2,1)}, bf16[320,384]{1,0:T(8,128)(2,1)}, f32[12...) custom-call(s32[1]{0:T(128)} %bitcast.here_ref, ...), custom_call_target="tpu_custom_call" | custom-call | flops 7549747200 | bytes 20971520 | tf_op jit(solution)/shard_map/pallas_call | solution.py:426
  264.0 12.1 %shard_map.175 = (bf16[4,2,320,960]{3,2,1,0:T(8,128)(2,1)}, bf16[4,2,320,960]{3,2,1,0:T(8,128)(2,1)}) custom-call(s32[1]{0:T(128)} %bitcast.1.place_ref, bf16[1280,384]{1,0:T(8,128)(2,1)} %get-tuple-element.119.branch_grad, bf16[1280,384]{1,0:T(8,128)(2,1)} %get-tuple-element.120.attended, bf16[1280,384]{1,0:T(8,128)(2,1)} %get-tuple-element.121.normed_two, ...), custom_call_target="tpu_custom_call" | custom-call | flops 3774873600 | bytes 16777216 | tf_op jit(solution)/shard_map/pallas_call | solution.py:456
  276.1 34.2 %all_to_all.10 = bf16[16,80,384]{2,1,0:T(8,128)(2,1)S(1)} all-to-all(bf16[16,80,384]{2,1,0:T(8,128)(2,1)S(1)} %copy-done.5), channel_id=1, replica_groups=mesh['dp'=2,'row'=4,'col'=4] {'row','col'}, dimensions={0} | all-to-all | bytes 1966080 | tf_op jit(solution)/shard_map/all_to_all | solution.py:798
  312.0 9.3 %add_convert_fusion = bf16[4,2,320,960]{3,2,1,0:T(8,128)(2,1)} fusion(bf16[4,2,320,960]{3,2,1,0:T(8,128)(2,1)} %collective-permute-done.33, bf16[4,2,320,960]{3,2,1,0:T(8,128)(2,1)} %get-tuple-element.125), kind=kLoop, calls=%fused_computation | loop fusion | flops 9830400 | bytes 14745600 | tf_op jit(solution)/shard_map/convert_element_type | solution.py:813
  324.4 49.2 %shard_map.176 = (bf16[240,768]{1,0:T(8,128)(2,1)}, bf16[240,768]{1,0:T(8,128)(2,1)}, bf16[240,768]{1,0:T(8,128)(2,1)}, bf16[240,768]{1,0:T(8,128)(2,1)}, bf16[2...) custom-call(s32[24]{0:T(128)} %convert_reduce_fusion.starts_ref, ...), custom_call_target="tpu_custom_call" | custom-call | flops 38654705664 | bytes 16777216 | tf_op jit(solution)/shard_map/pallas_call | solution.py:227
  377.9 7.6 %collective-permute-done.39.refs_3_ = bf16[240,768]{1,0:T(8,128)(2,1)S(1)} collective-permute-done((bf16[240,768]{1,0:T(8,128)(2,1)}, bf16[240,768]{1,0:T(8,128)(2,1)S(1)}, u32[]{:S(2)}, u32[]{:S(2)}) %collective-permute-start.39) | collective-permute-done | bytes 368672 | tf_op jit(solution)/shard_map/ppermute | solution.py:632
  385.5 7.2 %collective-permute-done.38.refs_2_ = bf16[240,768]{1,0:T(8,128)(2,1)S(1)} collective-permute-done((bf16[240,768]{1,0:T(8,128)(2,1)}, bf16[240,768]{1,0:T(8,128)(2,1)S(1)}, u32[]{:S(2)}, u32[]{:S(2)}) %collective-permute-start.38) | collective-permute-done | bytes 368672 | tf_op jit(solution)/shard_map/ppermute | solution.py:632
  393.6 9.5 %shard_map.177 = (bf16[336,768]{1,0:T(8,128)(2,1)}, bf16[336,768]{1,0:T(8,128)(2,1)}, bf16[336,768]{1,0:T(8,128)(2,1)}, bf16[336,768]{1,0:T(8,128)(2,1)}, bf16[3...) custom-call(s32[1]{0:T(128)} %bitcast.here_ref, ...), custom_call_target="tpu_custom_call" | custom-call | flops 1887436800 | bytes 12582912 | tf_op jit(solution)/shard_map/pallas_call | solution.py:583
  403.1 5.4 collective-permute-start.40
  410.3 9.3 %shard_map.178 = (bf16[336,768]{1,0:T(8,128)(2,1)}, bf16[336,768]{1,0:T(8,128)(2,1)}, bf16[336,768]{1,0:T(8,128)(2,1)}, bf16[336,768]{1,0:T(8,128)(2,1)}, bf16[3...) custom-call(s32[1]{0:T(128)} %bitcast.here_ref, ...), custom_call_target="tpu_custom_call" | custom-call | flops 1887436800 | bytes 12582912 | tf_op jit(solution)/shard_map/pallas_call | solution.py:583
  419.7 3.8 collective-permute-start.51
  423.5 1.5 collective-permute-start.54
  426.5 5.3 collective-permute-done.40
  431.8 9.4 %shard_map.179 = (bf16[2,320,960]{2,1,0:T(8,128)(2,1)}, bf16[2,320,960]{2,1,0:T(8,128)(2,1)}, f32[1280,1]{1,0:T(8,128)}) custom-call(s32[1]{0:T(128)} %bitcast.1.place_ref, bf16[1280,960]{1,0:T(8,128)(2,1)} %get-tuple-element.116.whole_ref, bf16[1280,768]{1,0:T(8,128)(2,1)} %get-tuple-element.106.normed_ref.refs_0_, ...), custom_call_target="tpu_custom_call" | custom-call | flops 3774873600 | bytes 12582912 | tf_op jit(solution)/shard_map/pallas_call | solution.py:616
  443.3 4.4 collective-permute-start.41
  452.4 1.5 broadcast_in_dim.27
  455.8 9.5 %collective-permute-start.59 = (f32[2640]{0:T(1024)S(1)}, f32[2640]{0:T(1024)S(1)}, u32[]{:S(2)}, u32[]{:S(2)}) collective-permute-start(f32[2640]{0:T(1024)S(1)} %add.210), channel_id=1, source_target_pairs={{0,16},{16,0},{1,17},{17,1},{2,18},{18,2},{3,19},{19,3},{4,20},{20... | collective-permute-start | bytes 31688 | tf_op jit(solution)/shard_map/ppermute | solution.py:632
  467.0 7.5 %collective-permute-start.60 = (f32[2640]{0:T(1024)S(1)}, f32[2640]{0:T(1024)S(1)}, u32[]{:S(2)}, u32[]{:S(2)}) collective-permute-start(f32[2640]{0:T(1024)S(1)} %add.211), channel_id=1, source_target_pairs={{0,1},{1,0},{2,3},{3,2},{4,5},{5,4},{6,7},{7,6},{8,9},{9,8},{10,11... | collective-permute-start | bytes 31688 | tf_op jit(solution)/shard_map/ppermute | solution.py:632
  476.2 4.1 collective-permute-start.61
  484.7 2.9 collective-permute-start.52
  491.5 3.1 collective-permute-done.52
  496.5 4.9 collective-permute-done.46
  501.3 5.8 %collective-permute-start.53 = (bf16[336,768]{1,0:T(8,128)(2,1)}, bf16[336,768]{1,0:T(8,128)(2,1)}, u32[]{:S(2)}, u32[]{:S(2)}) collective-permute-start(bf16[336,768]{1,0:T(8,128)(2,1)} %add_convert_fusion.4), channel_id=1, source_target_pairs={{0,1},{1,2},{2,3},{4,5},{5,6},{6,7},{8,9},{9,10},{10,11},{12,13},{... | collective-permute-start | bytes 1548296 | tf_op jit(solution)/shard_map/ppermute | solution.py:655
  508.5 5.4 collective-permute-start.47
  513.8 1.5 collective-permute-start.50
  517.9 1.6 fusion.6
  519.5 2.1 collective-permute-start.62
  521.6 1.9 collective-permute-done.56
  524.9 4.1 collective-permute-done.50
  531.8 2.1 collective-permute-start.64
  533.8 1.7 fusion.4
  536.4 1.6 copy.82
  538.0 6.3 %collective-permute-done.64 = bf16[320,960]{1,0:T(8,128)(2,1)} collective-permute-done((bf16[320,960]{1,0:T(8,128)(2,1)}, bf16[320,960]{1,0:T(8,128)(2,1)}, u32[]{:S(2)}, u32[]{:S(2)}) %collective-permute-start.64) | collective-permute-done | bytes 614432 | tf_op jit(solution)/shard_map/ppermute | solution.py:632
  544.3 1.5 convert_add_fusion.1
  (266 shorter events, 81.7 us)
Async XLA Ops:
  7.2 90.3 %all-gather.3.cloned.1.call-start = ((), (), s32[]{:S(2)}) async-start(), calls=%async_computation.4 | async-start | bytes 1802240 | tf_op jit(solution)/shard_map/all_gather | solution.py:740
  19.7 25.6 %collective-permute-start.14 = (bf16[320,768]{1,0:T(8,128)(2,1)}, bf16[320,768]{1,0:T(8,128)(2,1)}, u32[]{:S(2)}, u32[]{:S(2)}) collective-permute-start(bf16[320,768]{1,0:T(8,128)(2,1)} %get-tuple-element.232.refs_0_), channel_id=1, source_target_pairs={{0,1},{1,2},{2,3},{4,5},{5,6},{6,7},{8,9},{9,10},{10,11},{12,13},{... | collective-permute-start | bytes 1474568 | tf_op jit(solution)/shard_map/ppermute | solution.py:691
  24.3 35.6 %collective-permute-start.17 = (bf16[320,768]{1,0:T(8,128)(2,1)}, bf16[320,768]{1,0:T(8,128)(2,1)}, u32[]{:S(2)}, u32[]{:S(2)}) collective-permute-start(bf16[320,768]{1,0:T(8,128)(2,1)} %get-tuple-element.232.refs_0_), channel_id=1, source_target_pairs={{1,0},{2,1},{3,2},{5,4},{6,5},{7,6},{9,8},{10,9},{11,10},{13,12},{... | collective-permute-start | bytes 1474568 | tf_op jit(solution)/shard_map/ppermute | solution.py:692
  25.6 45.0 %collective-permute-start.8 = (bf16[320,768]{1,0:T(8,128)(2,1)}, bf16[320,768]{1,0:T(8,128)(2,1)}, u32[]{:S(2)}, u32[]{:S(2)}) collective-permute-start(bf16[320,768]{1,0:T(8,128)(2,1)} %get-tuple-element.233.refs_0_), channel_id=1, source_target_pairs={{1,0},{2,1},{3,2},{5,4},{6,5},{7,6},{9,8},{10,9},{11,10},{13,12},{... | collective-permute-start | bytes 1474568 | tf_op jit(solution)/shard_map/ppermute | solution.py:692
  29.0 44.2 %collective-permute-start.1 = (bf16[320,960]{1,0:T(8,128)(2,1)S(1)}, bf16[320,960]{1,0:T(8,128)(2,1)S(1)}, u32[]{:S(2)}, u32[]{:S(2)}) collective-permute-start(bf16[320,960]{1,0:T(8,128)(2,1)S(1)} %copy.69.refs_0_), channel_id=1, source_target_pairs={{0,8},{4,12},{8,0},{12,4},{1,9},{5,13},{9,1},{13,5},{2,10},{6,14},... | collective-permute-start | bytes 1843208 | tf_op jit(solution)/shard_map/ppermute | solution.py:632
  30.6 41.3 %collective-permute-start.5 = (bf16[320,768]{1,0:T(8,128)(2,1)}, bf16[320,768]{1,0:T(8,128)(2,1)}, u32[]{:S(2)}, u32[]{:S(2)}) collective-permute-start(bf16[320,768]{1,0:T(8,128)(2,1)} %get-tuple-element.233.refs_0_), channel_id=1, source_target_pairs={{0,1},{1,2},{2,3},{4,5},{5,6},{6,7},{8,9},{9,10},{10,11},{12,13},{... | collective-permute-start | bytes 1474568 | tf_op jit(solution)/shard_map/ppermute | solution.py:691
  45.3 28.0 %collective-permute-start = (bf16[320,960]{1,0:T(8,128)(2,1)S(1)}, bf16[320,960]{1,0:T(8,128)(2,1)S(1)}, u32[]{:S(2)}, u32[]{:S(2)}) collective-permute-start(bf16[320,960]{1,0:T(8,128)(2,1)S(1)} %copy.69.refs_0_), channel_id=1, source_target_pairs={{0,4},{4,0},{8,12},{12,8},{1,5},{5,1},{9,13},{13,9},{2,6},{6,2},{1... | collective-permute-start | bytes 1843208 | tf_op jit(solution)/shard_map/ppermute | solution.py:632
  59.9 15.8 %collective-permute-start.15 = (bf16[320,768]{1,0:T(8,128)(2,1)}, bf16[320,768]{1,0:T(8,128)(2,1)}, u32[]{:S(2)}, u32[]{:S(2)}) collective-permute-start(bf16[320,768]{1,0:T(8,128)(2,1)} %collective-permute-done.14.refs_1_), channel_id=1, source_target_pairs={{1,2},{2,3},{5,6},{6,7},{9,10},{10,11},{13,14},{14,15},{17,18},{18... | collective-permute-start | bytes 1474568 | tf_op jit(solution)/shard_map/ppermute | solution.py:691
  70.6 16.4 %collective-permute-start.18 = (bf16[320,768]{1,0:T(8,128)(2,1)}, bf16[320,768]{1,0:T(8,128)(2,1)}, u32[]{:S(2)}, u32[]{:S(2)}) collective-permute-start(bf16[320,768]{1,0:T(8,128)(2,1)} %collective-permute-done.17.refs_4_), channel_id=1, source_target_pairs={{1,0},{2,1},{5,4},{6,5},{9,8},{10,9},{13,12},{14,13},{17,16},{18,1... | collective-permute-start | bytes 1474568 | tf_op jit(solution)/shard_map/ppermute | solution.py:692
  71.9 25.6 %collective-permute-start.9 = (bf16[320,768]{1,0:T(8,128)(2,1)}, bf16[320,768]{1,0:T(8,128)(2,1)}, u32[]{:S(2)}, u32[]{:S(2)}) collective-permute-start(bf16[320,768]{1,0:T(8,128)(2,1)} %collective-permute-done.8.refs_4_), channel_id=1, source_target_pairs={{1,0},{2,1},{5,4},{6,5},{9,8},{10,9},{13,12},{14,13},{17,16},{18,1... | collective-permute-start | bytes 1474568 | tf_op jit(solution)/shard_map/ppermute | solution.py:692
  73.2 27.1 %collective-permute-start.2 = (bf16[320,960]{1,0:T(8,128)(2,1)S(1)}, bf16[320,960]{1,0:T(8,128)(2,1)}, u32[]{:S(2)}, u32[]{:S(2)}) collective-permute-start(bf16[320,960]{1,0:T(8,128)(2,1)S(1)} %collective-permute-done.1.refs_2_), channel_id=1, source_target_pairs={{0,4},{4,0},{8,12},{12,8},{1,5},{5,1},{9,13},{13,9},{2,6},{6,2},{1... | collective-permute-start | bytes 1843208 | tf_op jit(solution)/shard_map/ppermute | solution.py:632
  74.3 24.7 %collective-permute-start.6 = (bf16[320,768]{1,0:T(8,128)(2,1)}, bf16[320,768]{1,0:T(8,128)(2,1)}, u32[]{:S(2)}, u32[]{:S(2)}) collective-permute-start(bf16[320,768]{1,0:T(8,128)(2,1)} %collective-permute-done.5.refs_1_), channel_id=1, source_target_pairs={{1,2},{2,3},{5,6},{6,7},{9,10},{10,11},{13,14},{14,15},{17,18},{18... | collective-permute-start | bytes 1474568 | tf_op jit(solution)/shard_map/ppermute | solution.py:691
  75.7 31.2 %collective-permute-start.16 = (bf16[320,768]{1,0:T(8,128)(2,1)}, bf16[320,768]{1,0:T(8,128)(2,1)}, u32[]{:S(2)}, u32[]{:S(2)}) collective-permute-start(bf16[320,768]{1,0:T(8,128)(2,1)} %collective-permute-done.15.refs_2_), channel_id=1, source_target_pairs={{2,3},{6,7},{10,11},{14,15},{18,19},{22,23},{26,27},{30,31}} | collective-permute-start | bytes 1474568 | tf_op jit(solution)/shard_map/ppermute | solution.py:691
  87.0 21.1 %collective-permute-start.19 = (bf16[320,768]{1,0:T(8,128)(2,1)}, bf16[320,768]{1,0:T(8,128)(2,1)}, u32[]{:S(2)}, u32[]{:S(2)}) collective-permute-start(bf16[320,768]{1,0:T(8,128)(2,1)} %collective-permute-done.18.refs_5_), channel_id=1, source_target_pairs={{1,0},{5,4},{9,8},{13,12},{17,16},{21,20},{25,24},{29,28}} | collective-permute-start | bytes 1474568 | tf_op jit(solution)/shard_map/ppermute | solution.py:692
  97.5 51.2 %collective-permute-start.26 = (bf16[4,176,960]{2,1,0:T(8,128)(2,1)}, bf16[4,176,960]{2,1,0:T(8,128)(2,1)}, u32[]{:S(2)}, u32[]{:S(2)}) collective-permute-start(bf16[4,176,960]{2,1,0:T(8,128)(2,1)} %bitcast.9.refs_0_), channel_id=1, source_target_pairs={{0,8},{4,12},{8,0},{12,4},{1,9},{5,13},{9,1},{13,5},{2,10},{6,14},... | collective-permute-start | bytes 4055048 | tf_op jit(solution)/shard_map/ppermute | solution.py:632
  99.0 17.4 %collective-permute-start.10 = (bf16[320,768]{1,0:T(8,128)(2,1)}, bf16[320,768]{1,0:T(8,128)(2,1)}, u32[]{:S(2)}, u32[]{:S(2)}) collective-permute-start(bf16[320,768]{1,0:T(8,128)(2,1)} %collective-permute-done.9.refs_5_), channel_id=1, source_target_pairs={{1,0},{5,4},{9,8},{13,12},{17,16},{21,20},{25,24},{29,28}} | collective-permute-start | bytes 1474568 | tf_op jit(solution)/shard_map/ppermute | solution.py:692
  100.3 16.4 %collective-permute-start.7 = (bf16[320,768]{1,0:T(8,128)(2,1)}, bf16[320,768]{1,0:T(8,128)(2,1)}, u32[]{:S(2)}, u32[]{:S(2)}) collective-permute-start(bf16[320,768]{1,0:T(8,128)(2,1)} %collective-permute-done.6.refs_2_), channel_id=1, source_target_pairs={{2,3},{6,7},{10,11},{14,15},{18,19},{22,23},{26,27},{30,31}} | collective-permute-start | bytes 1474568 | tf_op jit(solution)/shard_map/ppermute | solution.py:691
  114.9 9.5 %collective-permute-start.20 = (bf16[240,768]{1,0:T(8,128)(2,1)}, bf16[240,768]{1,0:T(8,128)(2,1)S(1)}, u32[]{:S(2)}, u32[]{:S(2)}) collective-permute-start(bf16[240,768]{1,0:T(8,128)(2,1)} %get-tuple-element.102), channel_id=1, source_target_pairs={{0,4},{4,0},{8,12},{12,8},{1,5},{5,1},{9,13},{13,9},{2,6},{6,2},{1... | collective-permute-start | bytes 1105928 | tf_op jit(solution)/shard_map/ppermute | solution.py:632
  114.9 25.3 %collective-permute-start.21 = (bf16[240,768]{1,0:T(8,128)(2,1)}, bf16[240,768]{1,0:T(8,128)(2,1)S(1)}, u32[]{:S(2)}, u32[]{:S(2)}) collective-permute-start(bf16[240,768]{1,0:T(8,128)(2,1)} %get-tuple-element.103), channel_id=1, source_target_pairs={{0,8},{4,12},{8,0},{12,4},{1,9},{5,13},{9,1},{13,5},{2,10},{6,14},... | collective-permute-start | bytes 1105928 | tf_op jit(solution)/shard_map/ppermute | solution.py:632
  116.5 30.7 %collective-permute-start.22 = (bf16[240,768]{1,0:T(8,128)(2,1)}, bf16[240,768]{1,0:T(8,128)(2,1)S(1)}, u32[]{:S(2)}, u32[]{:S(2)}) collective-permute-start(bf16[240,768]{1,0:T(8,128)(2,1)} %get-tuple-element.104), channel_id=1, source_target_pairs={{0,12},{4,8},{8,4},{12,0},{1,13},{5,9},{9,5},{13,1},{2,14},{6,10},... | collective-permute-start | bytes 1105928 | tf_op jit(solution)/shard_map/ppermute | solution.py:632
  123.5 25.7 %collective-permute-start.11 = (bf16[240,768]{1,0:T(8,128)(2,1)}, bf16[240,768]{1,0:T(8,128)(2,1)S(1)}, u32[]{:S(2)}, u32[]{:S(2)}) collective-permute-start(bf16[240,768]{1,0:T(8,128)(2,1)} %get-tuple-element.98), channel_id=1, source_target_pairs={{0,4},{4,0},{8,12},{12,8},{1,5},{5,1},{9,13},{13,9},{2,6},{6,2},{1... | collective-permute-start | bytes 1105928 | tf_op jit(solution)/shard_map/ppermute | solution.py:632
  124.4 29.4 %collective-permute-start.12 = (bf16[240,768]{1,0:T(8,128)(2,1)}, bf16[240,768]{1,0:T(8,128)(2,1)}, u32[]{:S(2)}, u32[]{:S(2)}) collective-permute-start(bf16[240,768]{1,0:T(8,128)(2,1)} %get-tuple-element.99), channel_id=1, source_target_pairs={{0,8},{4,12},{8,0},{12,4},{1,9},{5,13},{9,1},{13,5},{2,10},{6,14},... | collective-permute-start | bytes 1105928 | tf_op jit(solution)/shard_map/ppermute | solution.py:632
  140.1 16.6 %collective-permute-start.13 = (bf16[240,768]{1,0:T(8,128)(2,1)}, bf16[240,768]{1,0:T(8,128)(2,1)}, u32[]{:S(2)}, u32[]{:S(2)}) collective-permute-start(bf16[240,768]{1,0:T(8,128)(2,1)} %get-tuple-element.100), channel_id=1, source_target_pairs={{0,12},{4,8},{8,4},{12,0},{1,13},{5,9},{9,5},{13,1},{2,14},{6,10},... | collective-permute-start | bytes 1105928 | tf_op jit(solution)/shard_map/ppermute | solution.py:632
  147.2 51.7 %collective-permute-start.23 = (bf16[4,176,960]{2,1,0:T(8,128)(2,1)}, bf16[4,176,960]{2,1,0:T(8,128)(2,1)}, u32[]{:S(2)}, u32[]{:S(2)}) collective-permute-start(bf16[4,176,960]{2,1,0:T(8,128)(2,1)} %bitcast.9.refs_0_), channel_id=1, source_target_pairs={{0,16},{16,0},{1,17},{17,1},{2,18},{18,2},{3,19},{19,3},{4,20},{20... | collective-permute-start | bytes 4055048 | tf_op jit(solution)/shard_map/ppermute | solution.py:632
  148.7 64.1 %collective-permute-start.27 = (bf16[4,176,960]{2,1,0:T(8,128)(2,1)}, bf16[4,176,960]{2,1,0:T(8,128)(2,1)}, u32[]{:S(2)}, u32[]{:S(2)}) collective-permute-start(bf16[4,176,960]{2,1,0:T(8,128)(2,1)} %collective-permute-done.26.refs_4_), channel_id=1, source_target_pairs={{0,16},{16,0},{1,17},{17,1},{2,18},{18,2},{3,19},{19,3},{4,20},{20... | collective-permute-start | bytes 4055048 | tf_op jit(solution)/shard_map/ppermute | solution.py:632
  193.1 45.6 %all-to-all-start = ((bf16[16,80,384]{2,1,0:T(8,128)(2,1)}), bf16[16,80,384]{2,1,0:T(8,128)(2,1)}, u32[]{:S(2)}, u32[]{:S(2)}) async-start(bf16[16,80,384]{2,1,0:T(8,128)(2,1)} %bitcast.6), calls=%async_computation | async-start | bytes 1966080 | tf_op jit(solution)/shard_map/all_to_all | solution.py:768
  197.4 318.0 %reduce-scatter.2.cloned.1.call-start = ((), (), s32[]{:S(2)}) async-start(), calls=%async_computation.3 | async-start | bytes 6553600 | tf_op jit(solution)/shard_map/reduce_scatter | solution.py:827
  197.9 18.2 %collective-permute-start.24 = (bf16[4,176,960]{2,1,0:T(8,128)(2,1)}, bf16[4,176,960]{2,1,0:T(8,128)(2,1)}, u32[]{:S(2)}, u32[]{:S(2)}) collective-permute-start(bf16[4,176,960]{2,1,0:T(8,128)(2,1)} %bitcast.9.refs_0_), channel_id=1, source_target_pairs={{0,4},{4,0},{8,12},{12,8},{1,5},{5,1},{9,13},{13,9},{2,6},{6,2},{1... | collective-permute-start | bytes 4055048 | tf_op jit(solution)/shard_map/ppermute | solution.py:632
  198.9 17.3 %collective-permute-start.25 = (bf16[4,176,960]{2,1,0:T(8,128)(2,1)}, bf16[4,176,960]{2,1,0:T(8,128)(2,1)}, u32[]{:S(2)}, u32[]{:S(2)}) collective-permute-start(bf16[4,176,960]{2,1,0:T(8,128)(2,1)} %collective-permute-done.23.refs_1_), channel_id=1, source_target_pairs={{0,4},{4,0},{8,12},{12,8},{1,5},{5,1},{9,13},{13,9},{2,6},{6,2},{1... | collective-permute-start | bytes 4055048 | tf_op jit(solution)/shard_map/ppermute | solution.py:632
  199.0 25.9 %collective-permute-start.28 = (bf16[4,176,960]{2,1,0:T(8,128)(2,1)}, bf16[4,176,960]{2,1,0:T(8,128)(2,1)}, u32[]{:S(2)}, u32[]{:S(2)}) collective-permute-start(bf16[4,176,960]{2,1,0:T(8,128)(2,1)} %collective-permute-done.26.refs_4_), channel_id=1, source_target_pairs={{0,4},{4,0},{8,12},{12,8},{1,5},{5,1},{9,13},{13,9},{2,6},{6,2},{1... | collective-permute-start | bytes 4055048 | tf_op jit(solution)/shard_map/ppermute | solution.py:632
  212.7 12.2 %collective-permute-start.29 = (bf16[4,176,960]{2,1,0:T(8,128)(2,1)}, bf16[4,176,960]{2,1,0:T(8,128)(2,1)}, u32[]{:S(2)}, u32[]{:S(2)}) collective-permute-start(bf16[4,176,960]{2,1,0:T(8,128)(2,1)} %collective-permute-done.27.refs_5_), channel_id=1, source_target_pairs={{0,4},{4,0},{8,12},{12,8},{1,5},{5,1},{9,13},{13,9},{2,6},{6,2},{1... | collective-permute-start | bytes 4055048 | tf_op jit(solution)/shard_map/ppermute | solution.py:632
  215.5 19.9 %collective-permute-start.30 = (bf16[320,384]{1,0:T(8,128)(2,1)}, bf16[320,384]{1,0:T(8,128)(2,1)S(1)}, u32[]{:S(2)}, u32[]{:S(2)}) collective-permute-start(bf16[320,384]{1,0:T(8,128)(2,1)} %get-tuple-element.226), channel_id=1, source_target_pairs={{0,1},{1,2},{2,3},{3,0},{4,5},{5,6},{6,7},{7,4},{8,9},{9,10},{10,1... | collective-permute-start | bytes 737288 | tf_op jit(solution)/shard_map/ppermute | solution.py:700
  216.2 22.5 %collective-permute-start.31 = (bf16[320,384]{1,0:T(8,128)(2,1)S(1)}, bf16[320,384]{1,0:T(8,128)(2,1)S(1)}, u32[]{:S(2)}, u32[]{:S(2)}) collective-permute-start(bf16[320,384]{1,0:T(8,128)(2,1)S(1)} %get-tuple-element.225), channel_id=1, source_target_pairs={{0,2},{1,3},{2,0},{3,1},{4,6},{5,7},{6,4},{7,5},{8,10},{9,11},{10,... | collective-permute-start | bytes 737288 | tf_op jit(solution)/shard_map/ppermute | solution.py:700
  216.2 22.5 %collective-permute-start.32 = (bf16[320,384]{1,0:T(8,128)(2,1)S(1)}, bf16[320,384]{1,0:T(8,128)(2,1)S(1)}, u32[]{:S(2)}, u32[]{:S(2)}) collective-permute-start(bf16[320,384]{1,0:T(8,128)(2,1)S(1)} %get-tuple-element.224), channel_id=1, source_target_pairs={{0,3},{1,0},{2,1},{3,2},{4,7},{5,4},{6,5},{7,6},{8,11},{9,8},{10,9... | collective-permute-start | bytes 737288 | tf_op jit(solution)/shard_map/ppermute | solution.py:700
  276.1 35.9 %collective-permute-start.33 = (bf16[4,2,320,960]{3,2,1,0:T(8,128)(2,1)}, bf16[4,2,320,960]{3,2,1,0:T(8,128)(2,1)}, u32[]{:S(2)}, u32[]{:S(2)}) collective-permute-start(bf16[4,2,320,960]{3,2,1,0:T(8,128)(2,1)} %get-tuple-element.126), channel_id=1, source_target_pairs={{0,4},{4,0},{8,12},{12,8},{1,5},{5,1},{9,13},{13,9},{2,6},{6,2},{1... | collective-permute-start | bytes 14745608 | tf_op jit(solution)/shard_map/ppermute | solution.py:632
  322.3 51.3 %collective-permute-start.36 = (bf16[320,384]{1,0:T(8,128)(2,1)S(1)}, bf16[320,384]{1,0:T(8,128)(2,1)S(1)}, u32[]{:S(2)}, u32[]{:S(2)}) collective-permute-start(bf16[320,384]{1,0:T(8,128)(2,1)S(1)} %copy-done.42), channel_id=1, source_target_pairs={{0,3},{1,0},{2,1},{3,2},{4,7},{5,4},{6,5},{7,6},{8,11},{9,8},{10,9... | collective-permute-start | bytes 737288 | tf_op jit(solution)/shard_map/ppermute | solution.py:700
  323.1 50.5 %collective-permute-start.35 = (bf16[320,384]{1,0:T(8,128)(2,1)S(1)}, bf16[320,384]{1,0:T(8,128)(2,1)S(1)}, u32[]{:S(2)}, u32[]{:S(2)}) collective-permute-start(bf16[320,384]{1,0:T(8,128)(2,1)S(1)} %copy-done.41), channel_id=1, source_target_pairs={{0,2},{1,3},{2,0},{3,1},{4,6},{5,7},{6,4},{7,5},{8,10},{9,11},{10,... | collective-permute-start | bytes 737288 | tf_op jit(solution)/shard_map/ppermute | solution.py:700
  323.6 50.0 %collective-permute-start.34 = (bf16[320,384]{1,0:T(8,128)(2,1)S(1)}, bf16[320,384]{1,0:T(8,128)(2,1)S(1)}, u32[]{:S(2)}, u32[]{:S(2)}) collective-permute-start(bf16[320,384]{1,0:T(8,128)(2,1)S(1)} %copy-done.40), channel_id=1, source_target_pairs={{0,1},{1,2},{2,3},{3,0},{4,5},{5,6},{6,7},{7,4},{8,9},{9,10},{10,1... | collective-permute-start | bytes 737288 | tf_op jit(solution)/shard_map/ppermute | solution.py:700
  374.4 11.1 %collective-permute-start.39 = (bf16[240,768]{1,0:T(8,128)(2,1)}, bf16[240,768]{1,0:T(8,128)(2,1)S(1)}, u32[]{:S(2)}, u32[]{:S(2)}) collective-permute-start(bf16[240,768]{1,0:T(8,128)(2,1)} %get-tuple-element.142), channel_id=1, source_target_pairs={{0,12},{4,8},{8,4},{12,0},{1,13},{5,9},{9,5},{13,1},{2,14},{6,10},... | collective-permute-start | bytes 1105928 | tf_op jit(solution)/shard_map/ppermute | solution.py:632
  374.6 18.1 %collective-permute-start.38 = (bf16[240,768]{1,0:T(8,128)(2,1)}, bf16[240,768]{1,0:T(8,128)(2,1)S(1)}, u32[]{:S(2)}, u32[]{:S(2)}) collective-permute-start(bf16[240,768]{1,0:T(8,128)(2,1)} %get-tuple-element.140), channel_id=1, source_target_pairs={{0,8},{4,12},{8,0},{12,4},{1,9},{5,13},{9,1},{13,5},{2,10},{6,14},... | collective-permute-start | bytes 1105928 | tf_op jit(solution)/shard_map/ppermute | solution.py:632
  375.6 17.2 %collective-permute-start.37 = (bf16[240,768]{1,0:T(8,128)(2,1)}, bf16[240,768]{1,0:T(8,128)(2,1)S(1)}, u32[]{:S(2)}, u32[]{:S(2)}) collective-permute-start(bf16[240,768]{1,0:T(8,128)(2,1)} %get-tuple-element.138), channel_id=1, source_target_pairs={{0,4},{4,0},{8,12},{12,8},{1,5},{5,1},{9,13},{13,9},{2,6},{6,2},{1... | collective-permute-start | bytes 1105928 | tf_op jit(solution)/shard_map/ppermute | solution.py:632
  376.3 33.3 %collective-permute-start.44 = (bf16[240,768]{1,0:T(8,128)(2,1)}, bf16[240,768]{1,0:T(8,128)(2,1)S(1)}, u32[]{:S(2)}, u32[]{:S(2)}) collective-permute-start(bf16[240,768]{1,0:T(8,128)(2,1)} %get-tuple-element.160), channel_id=1, source_target_pairs={{0,12},{4,8},{8,4},{12,0},{1,13},{5,9},{9,5},{13,1},{2,14},{6,10},... | collective-permute-start | bytes 1105928 | tf_op jit(solution)/shard_map/ppermute | solution.py:632
  377.0 32.6 %collective-permute-start.43 = (bf16[240,768]{1,0:T(8,128)(2,1)}, bf16[240,768]{1,0:T(8,128)(2,1)}, u32[]{:S(2)}, u32[]{:S(2)}) collective-permute-start(bf16[240,768]{1,0:T(8,128)(2,1)} %get-tuple-element.158), channel_id=1, source_target_pairs={{0,8},{4,12},{8,0},{12,4},{1,9},{5,13},{9,1},{13,5},{2,10},{6,14},... | collective-permute-start | bytes 1105928 | tf_op jit(solution)/shard_map/ppermute | solution.py:632
  385.5 24.1 %collective-permute-start.42 = (bf16[240,768]{1,0:T(8,128)(2,1)}, bf16[240,768]{1,0:T(8,128)(2,1)}, u32[]{:S(2)}, u32[]{:S(2)}) collective-permute-start(bf16[240,768]{1,0:T(8,128)(2,1)} %get-tuple-element.156), channel_id=1, source_target_pairs={{0,4},{4,0},{8,12},{12,8},{1,5},{5,1},{9,13},{13,9},{2,6},{6,2},{1... | collective-permute-start | bytes 1105928 | tf_op jit(solution)/shard_map/ppermute | solution.py:632
  403.1 28.8 %collective-permute-start.40 = (bf16[336,768]{1,0:T(8,128)(2,1)}, bf16[336,768]{1,0:T(8,128)(2,1)S(1)}, u32[]{:S(2)}, u32[]{:S(2)}) collective-permute-start(bf16[336,768]{1,0:T(8,128)(2,1)} %get-tuple-element.143), channel_id=1, source_target_pairs={{0,1},{4,5},{8,9},{12,13},{16,17},{20,21},{24,25},{28,29}} | collective-permute-start | bytes 1548296 | tf_op jit(solution)/shard_map/ppermute | solution.py:655
  419.7 29.2 %collective-permute-start.51 = (bf16[336,768]{1,0:T(8,128)(2,1)}, bf16[336,768]{1,0:T(8,128)(2,1)}, u32[]{:S(2)}, u32[]{:S(2)}) collective-permute-start(bf16[336,768]{1,0:T(8,128)(2,1)} %get-tuple-element.172), channel_id=1, source_target_pairs={{0,1},{4,5},{8,9},{12,13},{16,17},{20,21},{24,25},{28,29}} | collective-permute-start | bytes 1548296 | tf_op jit(solution)/shard_map/ppermute | solution.py:655
  423.5 27.3 %collective-permute-start.54 = (bf16[336,768]{1,0:T(8,128)(2,1)}, bf16[336,768]{1,0:T(8,128)(2,1)}, u32[]{:S(2)}, u32[]{:S(2)}) collective-permute-start(bf16[336,768]{1,0:T(8,128)(2,1)} %get-tuple-element.177), channel_id=1, source_target_pairs={{3,2},{7,6},{11,10},{15,14},{19,18},{23,22},{27,26},{31,30}} | collective-permute-start | bytes 1548296 | tf_op jit(solution)/shard_map/ppermute | solution.py:656
  425.0 18.3 %collective-permute-start.48 = (bf16[336,768]{1,0:T(8,128)(2,1)}, bf16[336,768]{1,0:T(8,128)(2,1)}, u32[]{:S(2)}, u32[]{:S(2)}) collective-permute-start(bf16[336,768]{1,0:T(8,128)(2,1)} %get-tuple-element.167), channel_id=1, source_target_pairs={{3,2},{7,6},{11,10},{15,14},{19,18},{23,22},{27,26},{31,30}} | collective-permute-start | bytes 1548296 | tf_op jit(solution)/shard_map/ppermute | solution.py:656
  441.2 43.6 %collective-permute-start.45 = (bf16[2,320,960]{2,1,0:T(8,128)(2,1)}, bf16[2,320,960]{2,1,0:T(8,128)(2,1)}, u32[]{:S(2)}, u32[]{:S(2)}) collective-permute-start(bf16[2,320,960]{2,1,0:T(8,128)(2,1)} %get-tuple-element.163), channel_id=1, source_target_pairs={{0,4},{4,0},{8,12},{12,8},{1,5},{5,1},{9,13},{13,9},{2,6},{6,2},{1... | collective-permute-start | bytes 3686408 | tf_op jit(solution)/shard_map/ppermute | solution.py:632
  442.6 9.4 %collective-permute-start.57 = (f32[2640]{0:T(1024)S(1)}, f32[2640]{0:T(1024)S(1)}, u32[]{:S(2)}, u32[]{:S(2)}) collective-permute-start(f32[2640]{0:T(1024)S(1)} %maximum_reduce_fusion), channel_id=1, source_target_pairs={{0,4},{4,0},{8,12},{12,8},{1,5},{5,1},{9,13},{13,9},{2,6},{6,2},{1... | collective-permute-start | bytes 31688 | tf_op jit(solution)/shard_map/ppermute | solution.py:632
  443.3 40.5 %collective-permute-start.41 = (bf16[336,768]{1,0:T(8,128)(2,1)S(1)}, bf16[336,768]{1,0:T(8,128)(2,1)S(1)}, u32[]{:S(2)}, u32[]{:S(2)}) collective-permute-start(bf16[336,768]{1,0:T(8,128)(2,1)S(1)} %add_convert_fusion.9), channel_id=1, source_target_pairs={{0,1},{1,2},{4,5},{5,6},{8,9},{9,10},{12,13},{13,14},{16,17},{17,1... | collective-permute-start | bytes 1548296 | tf_op jit(solution)/shard_map/ppermute | solution.py:655
  448.9 41.7 %collective-permute-start.49 = (bf16[336,768]{1,0:T(8,128)(2,1)S(1)}, bf16[336,768]{1,0:T(8,128)(2,1)S(1)}, u32[]{:S(2)}, u32[]{:S(2)}) collective-permute-start(bf16[336,768]{1,0:T(8,128)(2,1)S(1)} %add_convert_fusion.7), channel_id=1, source_target_pairs={{2,1},{3,2},{6,5},{7,6},{10,9},{11,10},{14,13},{15,14},{18,17},{19... | collective-permute-start | bytes 1548296 | tf_op jit(solution)/shard_map/ppermute | solution.py:656
  455.8 11.1 %collective-permute-start.59 = (f32[2640]{0:T(1024)S(1)}, f32[2640]{0:T(1024)S(1)}, u32[]{:S(2)}, u32[]{:S(2)}) collective-permute-start(f32[2640]{0:T(1024)S(1)} %add.210), channel_id=1, source_target_pairs={{0,16},{16,0},{1,17},{17,1},{2,18},{18,2},{3,19},{19,3},{4,20},{20... | collective-permute-start | bytes 31688 | tf_op jit(solution)/shard_map/ppermute | solution.py:632
  467.0 9.2 %collective-permute-start.60 = (f32[2640]{0:T(1024)S(1)}, f32[2640]{0:T(1024)S(1)}, u32[]{:S(2)}, u32[]{:S(2)}) collective-permute-start(f32[2640]{0:T(1024)S(1)} %add.211), channel_id=1, source_target_pairs={{0,1},{1,0},{2,3},{3,2},{4,5},{5,4},{6,7},{7,6},{8,9},{9,8},{10,11... | collective-permute-start | bytes 31688 | tf_op jit(solution)/shard_map/ppermute | solution.py:632
  476.2 5.8 %collective-permute-start.61 = (f32[2640]{0:T(1024)S(1)}, f32[2640]{0:T(1024)S(1)}, u32[]{:S(2)}, u32[]{:S(2)}) collective-permute-start(f32[2640]{0:T(1024)S(1)} %add.212), channel_id=1, source_target_pairs={{0,2},{1,3},{2,0},{3,1},{4,6},{5,7},{6,4},{7,5},{8,10},{9,11},{10,... | collective-permute-start | bytes 31688 | tf_op jit(solution)/shard_map/ppermute | solution.py:632
  484.7 9.8 %collective-permute-start.52 = (bf16[336,768]{1,0:T(8,128)(2,1)S(1)}, bf16[336,768]{1,0:T(8,128)(2,1)S(1)}, u32[]{:S(2)}, u32[]{:S(2)}) collective-permute-start(bf16[336,768]{1,0:T(8,128)(2,1)S(1)} %add_convert_fusion.5), channel_id=1, source_target_pairs={{0,1},{1,2},{4,5},{5,6},{8,9},{9,10},{12,13},{13,14},{16,17},{17,1... | collective-permute-start | bytes 1548296 | tf_op jit(solution)/shard_map/ppermute | solution.py:655
  489.0 12.3 %collective-permute-start.46 = (bf16[320,960]{1,0:T(8,128)(2,1)S(1)}, bf16[320,960]{1,0:T(8,128)(2,1)}, u32[]{:S(2)}, u32[]{:S(2)}) collective-permute-start(bf16[320,960]{1,0:T(8,128)(2,1)S(1)} %fusion.8), channel_id=1, source_target_pairs={{0,8},{4,12},{8,0},{12,4},{1,9},{5,13},{9,1},{13,5},{2,10},{6,14},... | collective-permute-start | bytes 1843208 | tf_op jit(solution)/shard_map/ppermute | solution.py:632
  501.3 18.2 %collective-permute-start.53 = (bf16[336,768]{1,0:T(8,128)(2,1)}, bf16[336,768]{1,0:T(8,128)(2,1)}, u32[]{:S(2)}, u32[]{:S(2)}) collective-permute-start(bf16[336,768]{1,0:T(8,128)(2,1)} %add_convert_fusion.4), channel_id=1, source_target_pairs={{0,1},{1,2},{2,3},{4,5},{5,6},{6,7},{8,9},{9,10},{10,11},{12,13},{... | collective-permute-start | bytes 1548296 | tf_op jit(solution)/shard_map/ppermute | solution.py:655
  507.2 16.4 %collective-permute-start.56 = (bf16[336,768]{1,0:T(8,128)(2,1)}, bf16[336,768]{1,0:T(8,128)(2,1)}, u32[]{:S(2)}, u32[]{:S(2)}) collective-permute-start(bf16[336,768]{1,0:T(8,128)(2,1)} %add_convert_fusion.2), channel_id=1, source_target_pairs={{1,0},{2,1},{3,2},{5,4},{6,5},{7,6},{9,8},{10,9},{11,10},{13,12},{... | collective-permute-start | bytes 1548296 | tf_op jit(solution)/shard_map/ppermute | solution.py:656
  508.5 16.4 %collective-permute-start.47 = (bf16[336,768]{1,0:T(8,128)(2,1)}, bf16[336,768]{1,0:T(8,128)(2,1)}, u32[]{:S(2)}, u32[]{:S(2)}) collective-permute-start(bf16[336,768]{1,0:T(8,128)(2,1)} %add_convert_fusion.8), channel_id=1, source_target_pairs={{0,1},{1,2},{2,3},{4,5},{5,6},{6,7},{8,9},{9,10},{10,11},{12,13},{... | collective-permute-start | bytes 1548296 | tf_op jit(solution)/shard_map/ppermute | solution.py:655
  513.8 15.2 %collective-permute-start.50 = (bf16[336,768]{1,0:T(8,128)(2,1)}, bf16[336,768]{1,0:T(8,128)(2,1)}, u32[]{:S(2)}, u32[]{:S(2)}) collective-permute-start(bf16[336,768]{1,0:T(8,128)(2,1)} %add_convert_fusion.6), channel_id=1, source_target_pairs={{1,0},{2,1},{3,2},{5,4},{6,5},{7,6},{9,8},{10,9},{11,10},{13,12},{... | collective-permute-start | bytes 1548296 | tf_op jit(solution)/shard_map/ppermute | solution.py:656
  516.6 14.0 %collective-permute-start.63 = (bf16[320,960]{1,0:T(8,128)(2,1)S(1)}, bf16[320,960]{1,0:T(8,128)(2,1)S(1)}, u32[]{:S(2)}, u32[]{:S(2)}) collective-permute-start(bf16[320,960]{1,0:T(8,128)(2,1)S(1)} %slice_bitcast_fusion), channel_id=1, source_target_pairs={{0,8},{4,12},{8,0},{12,4},{1,9},{5,13},{9,1},{13,5},{2,10},{6,14},... | collective-permute-start | bytes 1843208 | tf_op jit(solution)/shard_map/ppermute | solution.py:632
  519.5 16.1 %collective-permute-start.62 = (bf16[320,960]{1,0:T(8,128)(2,1)S(1)}, bf16[320,960]{1,0:T(8,128)(2,1)S(1)}, u32[]{:S(2)}, u32[]{:S(2)}) collective-permute-start(bf16[320,960]{1,0:T(8,128)(2,1)S(1)} %fusion.6), channel_id=1, source_target_pairs={{0,16},{16,0},{1,17},{17,1},{2,18},{18,2},{3,19},{19,3},{4,20},{20... | collective-permute-start | bytes 1843208 | tf_op jit(solution)/shard_map/ppermute | solution.py:632
  531.8 12.5 %collective-permute-start.64 = (bf16[320,960]{1,0:T(8,128)(2,1)}, bf16[320,960]{1,0:T(8,128)(2,1)}, u32[]{:S(2)}, u32[]{:S(2)}) collective-permute-start(bf16[320,960]{1,0:T(8,128)(2,1)} %fusion.5), channel_id=1, source_target_pairs={{0,16},{16,0},{1,17},{17,1},{2,18},{18,2},{3,19},{19,3},{4,20},{20... | collective-permute-start | bytes 1843208 | tf_op jit(solution)/shard_map/ppermute | solution.py:632
  (51 other events, 572.1 us)
Sparse Core Ops, SparseCore 0:
  17.8 47.8 all-gather.2
  321.5 118.8 reduce-scatter.1
